TPU v7x, 32 devices: a whole 2x2x4 slice. The times are simulated.
32 devices in a mesh: dm: 4 (over z), hv: 8 (over y, x, core).
Axes of the slice: x: 2, y: 2, z: 4, core: 2. Of those that a mesh axis runs over, the one named last changes fastest.
Arguments:
- tokens: bfloat16 [512, 16384], P('hv', 'dm'), may hold values from -64 to 64
- gate_weight: bfloat16 [16384, 13312], P('dm', 'hv'), may hold values from -0.046875 to 0.046875
- up_weight: bfloat16 [16384, 13312], P('dm', 'hv'), may hold values from -0.046875 to 0.046875
- down_weight: bfloat16 [13312, 16384], P('hv', 'dm'), may hold values from -0.0546875 to 0.0546875
- norm_gain: float32 [16384], P('dm'), may hold values from 0.1 to 1.9
- unembed: bfloat16 [16384, 32064], P('dm', 'hv'), may hold values from -8 to 8
- gold_ids: int32 [512], replicated, may hold values from 0 to 32063
- option_lengths: int32 [32], replicated, may hold values from 1 to 32, 512 in all
Outputs:
- token_logprob: float32 [512], replicated
- option_score: float32 [32], replicated
All inputs are finite; a program needn't handle non-finite values.
Results may differ from a plain program's by a relative error of at most 0.005.
Values may be sent and summed in bfloat16 or wider, within the bound.
No kernel may reach another device: no remote copies, remote signals or barrier semaphores. Data moves between devices by JAX's collectives and lax.ppermute only.
A program may use at most 128 MiB of HBM per device.

v0:
```python
import functools

import jax
import jax.numpy as jnp
from jax import lax
from jax.experimental import pallas as pl
from jax.experimental.pallas import tpu as pltpu
from jax.sharding import PartitionSpec as P

D = 16384
DOWN_CHUNKS = 2
VOCAB_TILE = 1024
F32 = jnp.float32
BF16 = jnp.bfloat16
MIB = 1 << 20
VMEM = pl.BlockSpec(memory_space=pltpu.VMEM)
SMEM = pl.BlockSpec(memory_space=pltpu.SMEM)
ANY = pl.BlockSpec(memory_space=pl.ANY)
DM_FIRST, DM_LAST, CORE, OFFSET = range(4)


def run(scalars, body, outs, arrays, after=None):
    ahead = [] if after is None else [after]

    def kernel(scalars, *refs):
        body(scalars, *refs[: len(arrays)], *refs[len(arrays) + len(ahead) :])

    return pl.pallas_call(
        kernel,
        out_shape=[jax.ShapeDtypeStruct(*out) for out in outs],
        in_specs=[SMEM, *[VMEM] * len(arrays), *[ANY] * len(ahead)],
        out_specs=[VMEM] * len(outs),
        compiler_params=pltpu.CompilerParams(vmem_limit_bytes=12 * MIB),
        cost_estimate=pl.CostEstimate(
            flops=0, bytes_accessed=2 * sum(a.size * a.dtype.itemsize for a in arrays), transcendentals=0
        ),
    )(scalars, *arrays, *ahead)


def tie(array, after):
    def body(array_ref, after_ref, out):
        pass

    return pl.pallas_call(
        body,
        out_shape=jax.ShapeDtypeStruct(array.shape, array.dtype),
        in_specs=[VMEM, ANY],
        out_specs=VMEM,
        input_output_aliases={0: 0},
        compiler_params=pltpu.CompilerParams(vmem_limit_bytes=12 * MIB),
    )(array, after)


def part(which, size):
    return pl.ds(pl.multiple_of(which * size, size), size)


def add(one, two, dtype):
    return (one.astype(F32) + two.astype(F32)).astype(dtype)


def columns_of(refs, rows):
    at = 0
    for ref in refs:
        yield at, ref[rows, :]
        at += ref.shape[1]


def pick(scalars, bit, arrays, after=None):
    size = arrays[0].shape[0] // 2
    width = pl.cdiv(sum(a.shape[1] for a in arrays), 128) * 128

    def body(scalars, *refs):
        for at, values in columns_of(refs[:-1], part(1 - scalars[bit], size)):
            refs[-1][:, pl.ds(at, values.shape[1])] = values

    return run(scalars, body, [((size, width), arrays[0].dtype)], arrays, after)[0]


def add_split(scalars, before, bit, arrays, got, after=None):
    def body(scalars, *refs):
        which = scalars[bit]
        size = got.shape[0] // 2
        for out, side in ((refs[-2], which), (refs[-1], 1 - which)):
            start = pl.multiple_of((2 * scalars[before] + side) * size, size)
            for at, values in columns_of(refs[: len(arrays)], pl.ds(start, size)):
                columns = pl.ds(at, values.shape[1])
                out[:, columns] = add(values, refs[len(arrays)][part(side, size), columns], out.dtype)

    return run(scalars, body, [((got.shape[0] // 2, got.shape[1]), got.dtype)] * 2, [*arrays, got], after)


def add_half(scalars, before, arrays, got, after=None):
    def body(scalars, *refs):
        size = got.shape[0]
        for at, values in columns_of(refs[: len(arrays)], part(scalars[before], size)):
            columns = pl.ds(at, values.shape[1])
            refs[-1][:, columns] = add(values, refs[len(arrays)][:, columns], got.dtype)

    return run(scalars, body, [(got.shape, got.dtype)], [*arrays, got], after)[0]


def join(scalars, bit, pairs, after=None):
    rows = sum(2 * own.shape[0] for own, _ in pairs)

    def body(scalars, *refs):
        which, at = scalars[bit], 0
        for i, (own, _) in enumerate(pairs):
            size = own.shape[0]
            for place, ref in ((which, refs[2 * i]), (1 - which, refs[2 * i + 1])):
                refs[-1][pl.ds(pl.multiple_of(at + place * size, 16), size), :] = ref[...]
            at += 2 * size

    own = pairs[0][0]
    return run(scalars, body, [((rows, own.shape[1]), own.dtype)], [a for pair in pairs for a in pair], after)[0]


def join_below(scalars, above, pairs):
    rows = above.shape[0] + sum(2 * own.shape[0] for own, _ in pairs)

    def body(scalars, above_ref, *refs):
        refs[-1][pl.ds(0, above.shape[0]), :] = above_ref[...]
        which, at = scalars[DM_FIRST], above.shape[0]
        for i, (own, _) in enumerate(pairs):
            size = own.shape[0]
            for place, ref in ((which, refs[2 * i]), (1 - which, refs[2 * i + 1])):
                refs[-1][pl.ds(pl.multiple_of(at + place * size, 16), size), :] = ref[...]
            at += 2 * size

    arrays = [above, *[array for pair in pairs for array in pair]]
    return run(scalars, body, [((rows, above.shape[1]), above.dtype)], arrays)[0]


def join_chips(scalars, own, got):
    size = own.shape[0] // 2

    def body(scalars, own_ref, got_ref, out):
        for side, ref in ((scalars[CORE], own_ref), (1 - scalars[CORE], got_ref)):
            for chip in range(2):
                rows = pl.ds(pl.multiple_of((2 * chip + side) * size, size), size)
                out[rows, :] = ref[pl.ds(chip * size, size), :]

    return run(scalars, body, [((4 * size, own.shape[1]), own.dtype)], [own, got])[0]


def activate(scalars, kept, got, after=None):
    def body(scalars, kept_ref, got_ref, out):
        width = out.shape[1]
        gate, up = (
            kept_ref[:, pl.ds(at, width)].astype(F32) + got_ref[:, pl.ds(at, width)].astype(F32) for at in (0, width)
        )
        out[...] = (gate / (1.0 + jnp.exp(-gate)) * up).astype(BF16)

    return run(scalars, body, [((kept.shape[0], kept.shape[1] // 2), BF16)], [kept, got], after)[0]


def other_core(scalars, ffn):
    size = ffn.shape[0] // 8

    def body(scalars, ref, out):
        for chip in range(4):
            start = pl.multiple_of((2 * chip + 1 - scalars[CORE]) * size, size)
            out[pl.ds(chip * size, size), :] = ref[pl.ds(start, size), :]

    return run(scalars, body, [((4 * size, ffn.shape[1]), ffn.dtype)], [ffn])[0]


def add_cores(scalars, ffn, got):
    size = ffn.shape[0] // 8

    def body(scalars, ref, got_ref, stay, go):
        core = scalars[CORE]
        for out, chips in ((stay, (0, 2 - core)), (go, (1 + core, 3))):
            for i, chip in enumerate(chips):
                rows = pl.ds(pl.multiple_of((2 * chip + core) * size, size), size)
                out[pl.ds(i * size, size), :] = add(ref[rows, :], got_ref[part(chip, size), :], out.dtype)

    return run(scalars, body, [((2 * size, ffn.shape[1]), ffn.dtype)] * 2, [ffn, got])


def add_halves(scalars, stay, got):
    size = stay.shape[0] // 2

    def body(scalars, stay_ref, got_ref, first, second):
        for at, out in ((0, first), (size, second)):
            rows = pl.ds(at, size)
            out[...] = add(stay_ref[rows, :], got_ref[rows, :], out.dtype)

    return run(scalars, body, [((size, stay.shape[1]), stay.dtype)] * 2, [stay, got])


def residual(scalars, mine, at, kept, got):
    width = kept.shape[1]

    def body(scalars, mine_ref, kept_ref, got_ref, out):
        ffn = kept_ref[...].astype(F32) + got_ref[...].astype(F32)
        out[...] = (mine_ref[:, pl.ds(at, width)].astype(F32) + ffn).astype(BF16)

    return run(scalars, body, [(kept.shape, BF16)], [mine, kept, got])[0]


def stack(scalars, first, second, after=None):
    size = first.shape[0]

    def body(scalars, first_ref, second_ref, out, chosen):
        out[pl.ds(0, size), :] = first_ref[...]
        out[pl.ds(size, size), :] = second_ref[...]
        if after is not None:
            chosen[...] = jnp.where(scalars[CORE] == 0, first_ref[...], second_ref[...])

    outs = [((2 * size, first.shape[1]), first.dtype), (first.shape if after is not None else (16, 128), first.dtype)]
    return run(scalars, body, outs, [first, second], after)


def moved(scalars, array, after):
    def body(scalars, ref, out):
        out[...] = ref[...]

    return run(scalars, body, [(array.shape, array.dtype)], [array], after)[0]


def by_chip(scalars, pair, got):
    size = pair.shape[0] // 2

    def body(scalars, pair_ref, got_ref, out):
        core = scalars[CORE]
        for ref, chips in ((pair_ref, (0, 2 - core)), (got_ref, (1 + core, 3))):
            for i, chip in enumerate(chips):
                out[part(chip, size), :] = ref[pl.ds(i * size, size), :]

    return run(scalars, body, [((4 * size, pair.shape[1]), pair.dtype)], [pair, got])[0]


def scaled(scalars, owns, gots, gain):
    size, width = owns[0].shape[0] // 4, owns[0].shape[1]

    def body(scalars, *refs):
        own_refs, got_refs, (gain_ref, out, squares) = refs[: len(owns)], refs[len(owns) : 2 * len(owns)], refs[-3:]
        for side, side_refs in ((scalars[CORE], own_refs), (1 - scalars[CORE], got_refs)):
            for at in range(0, 4 * size, 16):
                start = (2 * (at // size) + side) * size + at % size
                rows = pl.ds(pl.multiple_of(start, 16), 16)
                total = 0.0
                for i, ref in enumerate(side_refs):
                    wide = ref[pl.ds(at, 16), :].astype(F32)
                    columns = pl.ds(i * width, width)
                    out[rows, columns] = (wide * gain_ref[:, columns]).astype(BF16)
                    total += jnp.sum(wide * wide, axis=1, keepdims=True)
                squares[rows, :] = jnp.broadcast_to(total, (16, 128))

    outs = [((8 * size, width * len(owns)), BF16), ((8 * size, 128), F32)]
    return run(scalars, body, outs, [*owns, *gots, gain])


def row_scale(scalars, squares, more_squares, after):
    def body(scalars, squares_ref, more_ref, out):
        out[...] = lax.rsqrt((squares_ref[...] + more_ref[...]) / D + 1e-05)

    return run(scalars, body, [(squares.shape, F32)], [squares, more_squares], after)[0]


def row_stats(scalars, kepts, gots, scale, gold, first, columns, before=None, after=None):
    many, rows = len(kepts), kepts[0].shape[0]
    others = [] if before is None else [before]

    def body(scalars, *refs):
        scale_ref, gold_ref, *before_refs, out = refs[2 * many :]
        blocks = []
        for at in range(0, rows, 16):
            block = pl.ds(at, 16)
            start, chunks = first, []
            for kept, got in zip(refs[:many], refs[many : 2 * many]):
                logits = (kept[block, :].astype(F32) + got[block, :].astype(F32)) * scale_ref[block, :1]
                column = lax.broadcasted_iota(jnp.int32, logits.shape, 1) + start
                chunks.append((jnp.where(column < columns, logits, -jnp.inf), column))
                start += logits.shape[1]
            tops = [jnp.max(logits, axis=1, keepdims=True) for logits, _ in chunks]
            tops += [ref[block, 0:1] for ref in before_refs]
            top = functools.reduce(jnp.maximum, tops)
            total, picked = 0.0, 0.0
            for logits, column in chunks:
                total += jnp.sum(jnp.exp(logits - top), axis=1, keepdims=True)
                hit = (column + scalars[OFFSET] == gold_ref[block, :]) & (column < columns)
                picked += jnp.sum(jnp.where(hit, logits, 0.0), axis=1, keepdims=True)
            for ref in before_refs:
                total += ref[block, 1:2] * jnp.exp(ref[block, 0:1] - top)
                picked += ref[block, 2:3]
            lane = lax.broadcasted_iota(jnp.int32, (16, 128), 1)
            blocks.append(jnp.where(lane == 0, top, jnp.where(lane == 1, total, picked)))
        blocks = jnp.concatenate(blocks)
        out[...] = blocks if before is None else blocks.T[:8]

    outs = [((rows, 128) if before is None else (8, rows), F32)]
    return run(scalars, body, outs, [*kepts, *gots, scale, gold, *others], after)[0]


def swapper(n_dm, n_hv, on_dm, flip_of):
    pairs = []
    for dm in range(n_dm):
        for hv in range(n_hv):
            flip = flip_of(hv)
            to = (dm ^ flip, hv) if on_dm else (dm, hv ^ flip)
            pairs.append((dm * n_hv + hv, to[0] * n_hv + to[1]))
    return lambda array: lax.ppermute(array, ("dm", "hv"), pairs)


def on_blocks(
    tokens, gate_weight, up_weight, down_weight, norm_gain, unembed, gold_ids, option_lengths, *, n_dm, n_hv
):
    dm, hv = lax.axis_index("dm"), lax.axis_index("hv")
    core, chip = hv & 1, hv >> 1
    dm_first, dm_last = (dm >> core) & 1, (dm >> (1 - core)) & 1
    scalars = jnp.stack([dm_first, dm_last, core, hv * unembed.shape[1]]).astype(jnp.int32)
    z_first, z_last = (swapper(n_dm, n_hv, True, flip) for flip in (lambda hv: 1 << (hv & 1), lambda hv: 2 >> (hv & 1)))
    cores, x, y, xy_first, xy_last = (
        swapper(n_dm, n_hv, False, flip)
        for flip in (lambda hv: 1, lambda hv: 2, lambda hv: 4, lambda hv: 2 << (hv & 1), lambda hv: 4 >> (hv & 1))
    )
    gain = norm_gain[None, :]
    chip_rows = 2 * tokens.shape[0]

    def sums(piece):
        both = [jnp.dot(piece, weight, preferred_element_type=F32).astype(BF16) for weight in (gate_weight, up_weight)]
        return both, pick(scalars, DM_FIRST, both)

    tokens = jnp.where(dm < n_dm, tokens, 0)
    from_core, from_x, from_y = cores(tokens), x(tokens), y(tokens)
    both_0, sent_0 = sums(join(scalars, CORE, [(tokens, from_core)]))
    got_0 = z_first(sent_0)
    beside, chosen = stack(scalars, from_x, from_y, sent_0)
    across = xy_last(chosen)
    both_1, sent_1 = sums(join_chips(scalars, beside, cores(beside)))
    got_1 = z_first(sent_1)
    half_0 = add_half(scalars, DM_FIRST, both_0, got_0, sent_1)
    got_0 = z_last(half_0)
    across = moved(scalars, across, half_0)
    both_2, sent_2 = sums(join(scalars, CORE, [(across, cores(across))]))
    got_2 = z_first(sent_2)
    own_0 = activate(scalars, half_0, got_0, sent_2)
    got_0 = z_first(own_0)
    kept_1, sent_1 = add_split(scalars, DM_FIRST, DM_LAST, both_1, got_1, own_0)
    got_1 = z_last(sent_1)
    half_2 = add_half(scalars, DM_FIRST, both_2, got_2, kept_1)
    got_2 = z_last(half_2)
    own_1 = activate(scalars, kept_1, got_1, half_2)
    got_1 = z_last(own_1)
    whole_0 = join(scalars, DM_FIRST, [(own_0, got_0)], own_1)
    own_2 = activate(scalars, half_2, got_2, whole_0)
    got_2 = z_first(own_2)
    own_1 = join(scalars, DM_LAST, [(own_1, got_1)], own_2)
    hidden = join_below(scalars, whole_0, [(own_1, z_first(own_1)), (own_2, got_2)])
    owns, gots = [], []
    width = down_weight.shape[1] // DOWN_CHUNKS
    for at in range(0, down_weight.shape[1], width):
        ffn = jnp.dot(hidden, down_weight[:, at : at + width], preferred_element_type=F32).astype(BF16)
        stay, go = add_cores(scalars, ffn, cores(other_core(scalars, ffn)))
        stay, go = add_halves(scalars, stay, xy_first(go))
        resid = residual(scalars, tokens, at, stay, xy_last(go))
        pair, _ = stack(scalars, resid, xy_last(resid))
        owns.append(by_chip(scalars, pair, xy_first(pair)))
        gots.append(cores(owns[-1]))
    left, squares = scaled(scalars, owns, gots, gain)
    gold = lax.dynamic_slice_in_dim(gold_ids, (chip ^ (2 * dm_first + dm_last)) * chip_rows, chip_rows)[:, None]
    sent_squares = pick(scalars, DM_FIRST, [squares])
    got_squares = z_first(sent_squares)
    left = tie(left, sent_squares)
    kepts, gots, first, scale = [], [], None, None
    for at in range(0, unembed.shape[1], VOCAB_TILE):
        logits = jnp.dot(left, unembed[:, at : at + VOCAB_TILE], preferred_element_type=F32).astype(BF16)
        sent = pick(scalars, DM_FIRST, [logits])
        got = z_first(sent)
        if first is None:
            last, sent_squares = add_split(scalars, DM_FIRST, DM_LAST, [squares], got_squares, sent)
            kept_squares, got_squares = last, z_last(sent_squares)
        else:
            if scale is None:
                sent = scale = row_scale(scalars, kept_squares, got_squares, sent)
            last, sent = add_split(scalars, DM_FIRST, DM_LAST, *first, sent)
            kepts.append(last)
            gots.append(z_last(sent))
        first = ([logits], got)
        if at + VOCAB_TILE < unembed.shape[1]:
            left = tie(left, last)
    last, sent = add_split(scalars, DM_FIRST, DM_LAST, *first, last)
    columns = unembed.shape[1]
    stats = row_stats(scalars, kepts, gots, scale, gold, 0, columns, None, last)
    stats = row_stats(scalars, [last], [z_last(sent)], scale, gold, VOCAB_TILE * len(kepts), columns, stats)
    stats = stats[None]
    for bit, swap in ((dm_last, z_last), (dm_first, z_first)):
        got = swap(stats)
        stats = jnp.concatenate([jnp.where(bit == 0, stats, got), jnp.where(bit == 0, got, stats)])
    stats = stats.reshape(2, 2, 8, chip_rows)
    stats = jnp.where(chip & 1 == 0, stats, stats[:, ::-1])
    stats = jnp.where(chip >> 1 == 0, stats, stats[::-1])
    stats = lax.all_gather(stats.reshape(4, 8, chip_rows), "hv", axis=0)
    top = jnp.max(stats[:, :, 0], axis=0)
    total = jnp.sum(stats[:, :, 1] * jnp.exp(stats[:, :, 0] - top), axis=0)
    return (jnp.sum(stats[:, :, 2], axis=0) - top - jnp.log(total)).reshape(-1)


def on_any_mesh(
    tokens, gate_weight, up_weight, down_weight, norm_gain, unembed, gold_ids, option_lengths, *, n_dm, n_hv
):
    piece = lax.all_gather(tokens, "hv", axis=0, tiled=True)
    gate, up = (
        lax.psum_scatter(
            jnp.dot(piece, weight, preferred_element_type=F32), "dm", scatter_dimension=0, tiled=True
        )
        for weight in (gate_weight, up_weight)
    )
    hidden = lax.all_gather((jax.nn.silu(gate) * up).astype(BF16), "dm", axis=0, tiled=True)
    ffn = jnp.dot(hidden, down_weight, preferred_element_type=F32)
    ffn = lax.psum_scatter(ffn, "hv", scatter_dimension=0, tiled=True)
    resid = (tokens.astype(F32) + ffn).astype(BF16)
    wide = resid.astype(F32)
    squares = lax.psum(jnp.sum(wide * wide, axis=1), "dm")
    normed = (wide * lax.rsqrt(squares[:, None] / D + 1e-05) * norm_gain).astype(BF16)
    normed = lax.all_gather(normed, "hv", axis=0, tiled=True)
    logits = jnp.dot(normed, unembed, preferred_element_type=F32)
    logits = lax.psum_scatter(logits, "dm", scatter_dimension=0, tiled=True)
    rows = logits.shape[0]
    gold = lax.dynamic_slice_in_dim(gold_ids, lax.axis_index("dm") * rows, rows)
    hit = lax.broadcasted_iota(jnp.int32, logits.shape, 1) + lax.axis_index("hv") * unembed.shape[1] == gold[:, None]
    top = lax.pmax(jnp.max(logits, axis=1), "hv")
    total, gold = lax.psum(
        (jnp.sum(jnp.exp(logits - top[:, None]), axis=1), jnp.sum(jnp.where(hit, logits, 0.0), axis=1)), "hv"
    )
    return lax.all_gather(gold - top - jnp.log(total), "dm", axis=0, tiled=True)


def per_device(*args, n_dm, n_hv):
    rows = on_blocks if (n_dm, n_hv) == (4, 8) else on_any_mesh
    token_logprob = rows(*args, n_dm=n_dm, n_hv=n_hv)
    option_lengths = args[-1]
    ends = jnp.cumsum(option_lengths)
    starts = ends - option_lengths
    places = jnp.arange(token_logprob.shape[0], dtype=jnp.int32)
    member = ((places[None, :] >= starts[:, None]) & (places[None, :] < ends[:, None])).astype(F32)
    option_sums = jnp.dot(member, token_logprob, precision=lax.Precision.HIGHEST)
    option_score = option_sums / option_lengths.astype(F32)
    return (token_logprob, option_score)


def solution(mesh):
    placed = (
        P("hv", "dm"),
        P("dm", "hv"),
        P("dm", "hv"),
        P("hv", "dm"),
        P("dm"),
        P("dm", "hv"),
        P(),
        P(),
    )
    body = functools.partial(per_device, n_dm=mesh.shape["dm"], n_hv=mesh.shape["hv"])
    return jax.shard_map(
        body, mesh=mesh, in_specs=placed, out_specs=(P(), P()), check_vma=False
    )
```

profile of v0, /device:TPU:0, one launch (start us, length us, event | category | flops | bytes accessed | tf_op | source)
XLA Modules:
  0.0 293.4 jit_solution(16419994979810327809)
XLA Ops:
  7.1 7.1 %convolution_convert_fusion.4.refs_1_ = bf16[128,1664]{1,0:T(8,128)(2,1)S(1)} fusion(bf16[128,4096]{1,0:T(8,128)(2,1)S(1)} %shard_map.95, bf16[4096,1664]{1,0:T(8,128)(2,1)} %param.10), kind=kOutput, calls=%fused_computation.18 | convolution fusion | flops 1745043456 | bytes 15106048 | tf_op jit(solution)/shard_map/dot_general | solution.py:323
  27.4 7.3 %convolution_convert_fusion.1.refs_0_ = bf16[256,1664]{1,0:T(8,128)(2,1)S(1)} fusion(bf16[256,4096]{1,0:T(8,128)(2,1)S(1)} %shard_map.98, bf16[4096,1664]{1,0:T(8,128)(2,1)} %param.9), kind=kOutput, calls=%fused_computation.15 | convolution fusion | flops 3490086912 | bytes 16580608 | tf_op jit(solution)/shard_map/dot_general | solution.py:323
  43.3 7.1 %convolution_convert_fusion.3.refs_0_ = bf16[128,1664]{1,0:T(8,128)(2,1)S(1)} fusion(bf16[128,4096]{1,0:T(8,128)(2,1)S(1)} %shard_map.102, bf16[4096,1664]{1,0:T(8,128)(2,1)} %param.9), kind=kOutput, calls=%fused_computation.17 | convolution fusion | flops 1745043456 | bytes 15106048 | tf_op jit(solution)/shard_map/dot_general | solution.py:323
  51.9 6.8 %collective-permute-done.5.refs_1_ = bf16[64,3328]{1,0:T(8,128)(2,1)S(1)} collective-permute-done((bf16[64,3328]{1,0:T(8,128)(2,1)S(1)}, bf16[64,3328]{1,0:T(8,128)(2,1)S(1)}, u32[]{:S(2)}, u32[]{:S(2)}) %collective-permute-start.5) | collective-permute-done | bytes 426016 | tf_op jit(solution)/shard_map/ppermute | solution.py:304
  59.4 8.5 %collective-permute-done.9.refs_2_ = bf16[128,3328]{1,0:T(8,128)(2,1)S(1)} collective-permute-done((bf16[128,3328]{1,0:T(8,128)(2,1)S(1)}, bf16[128,3328]{1,0:T(8,128)(2,1)S(1)}, u32[]{:S(2)}, u32[]{:S(2)}) %collective-permute-start.9) | collective-permute-done | bytes 852000 | tf_op jit(solution)/shard_map/ppermute | solution.py:304
  70.9 5.3 %collective-permute-done.11.refs_2_ = bf16[64,3328]{1,0:T(8,128)(2,1)S(1)} collective-permute-done((bf16[64,3328]{1,0:T(8,128)(2,1)S(1)}, bf16[64,3328]{1,0:T(8,128)(2,1)S(1)}, u32[]{:S(2)}, u32[]{:S(2)}) %collective-permute-start.11) | collective-permute-done | bytes 426016 | tf_op jit(solution)/shard_map/ppermute | solution.py:304
  79.9 6.2 %collective-permute-done.10.refs_1_ = bf16[64,3328]{1,0:T(8,128)(2,1)S(1)} collective-permute-done((bf16[64,3328]{1,0:T(8,128)(2,1)S(1)}, bf16[64,3328]{1,0:T(8,128)(2,1)S(1)}, u32[]{:S(2)}, u32[]{:S(2)}) %collective-permute-start.10) | collective-permute-done | bytes 426016 | tf_op jit(solution)/shard_map/ppermute | solution.py:304
  91.6 4.6 %collective-permute-done.13.refs_1_ = bf16[64,3328]{1,0:T(8,128)(2,1)S(1)} collective-permute-done((bf16[64,3328]{1,0:T(8,128)(2,1)S(1)}, bf16[64,3328]{1,0:T(8,128)(2,1)S(1)}, u32[]{:S(2)}, u32[]{:S(2)}) %collective-permute-start.13) | collective-permute-done | bytes 426016 | tf_op jit(solution)/shard_map/ppermute | solution.py:304
  96.9 5.4 %collective-permute-done.12.refs_1_ = bf16[64,1664]{1,0:T(8,128)(2,1)S(1)} collective-permute-done((bf16[64,1664]{1,0:T(8,128)(2,1)S(1)}, bf16[64,1664]{1,0:T(8,128)(2,1)S(1)}, u32[]{:S(2)}, u32[]{:S(2)}) %collective-permute-start.12) | collective-permute-done | bytes 213024 | tf_op jit(solution)/shard_map/ppermute | solution.py:304
  106.3 12.4 %collective-permute-done.15.refs_4_ = bf16[64,1664]{1,0:T(8,128)(2,1)S(1)} collective-permute-done((bf16[64,1664]{1,0:T(8,128)(2,1)S(1)}, bf16[64,1664]{1,0:T(8,128)(2,1)S(1)}, u32[]{:S(2)}, u32[]{:S(2)}) %collective-permute-start.15) | collective-permute-done | bytes 213024 | tf_op jit(solution)/shard_map/ppermute | solution.py:304
  124.2 7.5 %collective-permute-start.21 = (bf16[256,2048]{1,0:T(8,128)(2,1)S(1)}, bf16[256,2048]{1,0:T(8,128)(2,1)S(1)}, u32[]{:S(2)}, u32[]{:S(2)}) collective-permute-start(bf16[256,2048]{1,0:T(8,128)(2,1)S(1)} %shard_map.118), channel_id=1, source_target_pairs={{0,1},{1,0},{2,3},{3,2},{4,5},{5,4},{6,7},{7,6},{8,9},{9,8},{10,11... | collective-permute-start | bytes 3145736 | tf_op jit(solution)/shard_map/ppermute | solution.py:304
  140.6 6.3 %collective-permute-done.22.refs_1_ = bf16[128,2048]{1,0:T(8,128)(2,1)S(1)} collective-permute-done((bf16[128,2048]{1,0:T(8,128)(2,1)S(1)}, bf16[128,2048]{1,0:T(8,128)(2,1)S(1)}, u32[]{:S(2)}, u32[]{:S(2)}) %collective-permute-start.22) | collective-permute-done | bytes 524320 | tf_op jit(solution)/shard_map/ppermute | solution.py:304
  148.1 7.0 %collective-permute-done.17.refs_1_ = bf16[128,2048]{1,0:T(8,128)(2,1)S(1)} collective-permute-done((bf16[128,2048]{1,0:T(8,128)(2,1)S(1)}, bf16[128,2048]{1,0:T(8,128)(2,1)S(1)}, u32[]{:S(2)}, u32[]{:S(2)}) %collective-permute-start.17) | collective-permute-done | bytes 524320 | tf_op jit(solution)/shard_map/ppermute | solution.py:304
  166.2 5.9 %collective-permute-done.19.refs_1_ = bf16[64,2048]{1,0:T(8,128)(2,1)S(1)} collective-permute-done((bf16[64,2048]{1,0:T(8,128)(2,1)S(1)}, bf16[64,2048]{1,0:T(8,128)(2,1)S(1)}, u32[]{:S(2)}, u32[]{:S(2)}) %collective-permute-start.19) | collective-permute-done | bytes 262176 | tf_op jit(solution)/shard_map/ppermute | solution.py:304
  176.0 6.4 %collective-permute-done.20.refs_1_ = bf16[128,2048]{1,0:T(8,128)(2,1)S(1)} collective-permute-done((bf16[128,2048]{1,0:T(8,128)(2,1)S(1)}, bf16[128,2048]{1,0:T(8,128)(2,1)S(1)}, u32[]{:S(2)}, u32[]{:S(2)}) %collective-permute-start.20) | collective-permute-done | bytes 524320 | tf_op jit(solution)/shard_map/ppermute | solution.py:304
  189.8 7.1 %fusion.21.refs_0_ = bf16[512,1024]{1,0:T(8,128)(2,1)S(1)} fusion(bf16[512,4096]{1,0:T(8,128)(2,1)S(1)} %shard_map.126.array_ref, bf16[4096,4008]{0,1:T(8,128)(2,1)} %param.13), kind=kOutput, calls=%fused_computation.21 | convolution fusion | flops 4295491584 | bytes 13631488 | tf_op jit(solution)/shard_map/dot_general | solution.py:369
  201.3 7.1 %fusion.24.refs_0_ = bf16[512,1024]{1,0:T(8,128)(2,1)S(1)} fusion(bf16[512,4096]{1,0:T(8,128)(2,1)S(1)} %shard_map.129.array_ref, bf16[4096,4008]{0,1:T(8,128)(2,1)} %param.13), kind=kOutput, calls=%fused_computation.22 | convolution fusion | flops 4295491584 | bytes 13631488 | tf_op jit(solution)/shard_map/dot_general | solution.py:369
  213.1 7.1 %fusion.27.refs_0_ = bf16[512,1024]{1,0:T(8,128)(2,1)S(1)} fusion(bf16[512,4096]{1,0:T(8,128)(2,1)S(1)} %shard_map.133.array_ref, bf16[4096,4008]{0,1:T(8,128)(2,1)} %param.13), kind=kOutput, calls=%fused_computation.23 | convolution fusion | flops 4295491584 | bytes 13631488 | tf_op jit(solution)/shard_map/dot_general | solution.py:369
  220.8 5.1 %collective-permute-start.33 = (bf16[256,1024]{1,0:T(8,128)(2,1)S(1)}, bf16[256,1024]{1,0:T(8,128)(2,1)S(1)}, u32[]{:S(2)}, u32[]{:S(2)}) collective-permute-start(bf16[256,1024]{1,0:T(8,128)(2,1)S(1)} %shard_map.134.refs_2_), channel_id=1, source_target_pairs={{0,8},{1,17},{2,10},{3,19},{4,12},{5,21},{6,14},{7,23},{8,0},{9,25... | collective-permute-start | bytes 1572872 | tf_op jit(solution)/shard_map/ppermute | solution.py:304
  226.6 7.3 %fusion.18.refs_0_ = bf16[512,936]{1,0:T(8,128)(2,1)S(1)} fusion(bf16[512,4096]{1,0:T(8,128)(2,1)S(1)} %shard_map.136, bf16[4096,4008]{0,1:T(8,128)(2,1)} %param.13), kind=kOutput, calls=%fused_computation.20 | convolution fusion | flops 3926347776 | bytes 12820480 | tf_op jit(solution)/shard_map/dot_general | solution.py:369
  241.0 22.9 %collective-permute-done.32.refs_1_ = bf16[256,1024]{1,0:T(8,128)(2,1)S(1)} collective-permute-done((bf16[256,1024]{1,0:T(8,128)(2,1)S(1)}, bf16[256,1024]{1,0:T(8,128)(2,1)S(1)}, u32[]{:S(2)}, u32[]{:S(2)}) %collective-permute-start.32) | collective-permute-done | bytes 524320 | tf_op jit(solution)/shard_map/ppermute | solution.py:304
  268.5 5.5 %collective-permute-done.34.refs_1_ = bf16[128,1024]{1,0:T(8,128)(2,1)S(1)} collective-permute-done((bf16[128,1024]{1,0:T(8,128)(2,1)S(1)}, bf16[128,1024]{1,0:T(8,128)(2,1)S(1)}, u32[]{:S(2)}, u32[]{:S(2)}) %collective-permute-start.34) | collective-permute-done | bytes 262176 | tf_op jit(solution)/shard_map/ppermute | solution.py:304
  276.4 4.5 %collective-permute-done.38 = f32[1,8,128]{2,1,0:T(8,128)S(1)} collective-permute-done((f32[1,8,128]{2,1,0:T(8,128)S(1)}, f32[1,8,128]{2,1,0:T(8,128)S(1)}, u32[]{:S(2)}, u32[]{:S(2)}) %collective-permute-start.38) | collective-permute-done | bytes 4128 | tf_op jit(solution)/shard_map/ppermute | solution.py:304
  284.6 7.9 %all_gather.3 = f32[8,4,8,128]{3,2,1,0:T(8,128)S(1)} all-gather(f32[1,4,8,128]{3,2,1,0:T(8,128)S(1)} %bitcast.49), channel_id=1, replica_groups=mesh['dm'=4,'hv'=8] {'hv'}, dimensions={0}, use_global_device_ids=true | all-gather | bytes 147456 | tf_op jit(solution)/shard_map/all_gather | solution.py:395
  (163 shorter events, 113.9 us)
Async XLA Ops:
  2.3 16.2 %collective-permute-start.2 = (bf16[64,4096]{1,0:T(8,128)(2,1)S(1)}, bf16[64,4096]{1,0:T(8,128)(2,1)S(1)}, u32[]{:S(2)}, u32[]{:S(2)}) collective-permute-start(bf16[64,4096]{1,0:T(8,128)(2,1)S(1)} %broadcast_select_fusion.refs_0_), channel_id=1, source_target_pairs={{0,2},{1,3},{2,0},{3,1},{4,6},{5,7},{6,4},{7,5},{8,10},{9,11},{10,... | collective-permute-start | bytes 1572872 | tf_op jit(solution)/shard_map/ppermute | solution.py:304
  4.8 14.0 %collective-permute-start.3 = (bf16[64,4096]{1,0:T(8,128)(2,1)S(1)}, bf16[64,4096]{1,0:T(8,128)(2,1)S(1)}, u32[]{:S(2)}, u32[]{:S(2)}) collective-permute-start(bf16[64,4096]{1,0:T(8,128)(2,1)S(1)} %broadcast_select_fusion.refs_0_), channel_id=1, source_target_pairs={{0,4},{1,5},{2,6},{3,7},{4,0},{5,1},{6,2},{7,3},{8,12},{9,13},{10,... | collective-permute-start | bytes 1572872 | tf_op jit(solution)/shard_map/ppermute | solution.py:304
  19.6 15.8 %collective-permute-start.1 = (bf16[64,3328]{1,0:T(8,128)(2,1)S(1)}, bf16[64,3328]{1,0:T(8,128)(2,1)S(1)}, u32[]{:S(2)}, u32[]{:S(2)}) collective-permute-start(bf16[64,3328]{1,0:T(8,128)(2,1)S(1)} %shard_map.96.refs_2_), channel_id=1, source_target_pairs={{0,8},{1,17},{2,10},{3,19},{4,12},{5,21},{6,14},{7,23},{8,0},{9,25... | collective-permute-start | bytes 1277960 | tf_op jit(solution)/shard_map/ppermute | solution.py:304
  21.2 14.9 %collective-permute-start.6 = (bf16[64,4096]{1,0:T(8,128)(2,1)S(1)}, bf16[64,4096]{1,0:T(8,128)(2,1)S(1)}, u32[]{:S(2)}, u32[]{:S(2)}) collective-permute-start(bf16[64,4096]{1,0:T(8,128)(2,1)S(1)} %get-tuple-element.29), channel_id=1, source_target_pairs={{0,4},{1,3},{2,6},{3,1},{4,0},{5,7},{6,2},{7,5},{8,12},{9,11},{10,... | collective-permute-start | bytes 1572872 | tf_op jit(solution)/shard_map/ppermute | solution.py:304
  36.7 22.0 %collective-permute-start.5 = (bf16[64,3328]{1,0:T(8,128)(2,1)S(1)}, bf16[64,3328]{1,0:T(8,128)(2,1)S(1)}, u32[]{:S(2)}, u32[]{:S(2)}) collective-permute-start(bf16[64,3328]{1,0:T(8,128)(2,1)S(1)} %shard_map.100.refs_1_.refs_0_), channel_id=1, source_target_pairs={{0,16},{1,9},{2,18},{3,11},{4,20},{5,13},{6,22},{7,15},{8,24},{9,1... | collective-permute-start | bytes 1277960 | tf_op jit(solution)/shard_map/ppermute | solution.py:304
  39.4 28.6 %collective-permute-start.9 = (bf16[128,3328]{1,0:T(8,128)(2,1)S(1)}, bf16[128,3328]{1,0:T(8,128)(2,1)S(1)}, u32[]{:S(2)}, u32[]{:S(2)}) collective-permute-start(bf16[128,3328]{1,0:T(8,128)(2,1)S(1)} %shard_map.99.refs_3_), channel_id=1, source_target_pairs={{0,8},{1,17},{2,10},{3,19},{4,12},{5,21},{6,14},{7,23},{8,0},{9,25... | collective-permute-start | bytes 2555912 | tf_op jit(solution)/shard_map/ppermute | solution.py:304
  50.9 25.2 %collective-permute-start.11 = (bf16[64,3328]{1,0:T(8,128)(2,1)S(1)}, bf16[64,3328]{1,0:T(8,128)(2,1)S(1)}, u32[]{:S(2)}, u32[]{:S(2)}) collective-permute-start(bf16[64,3328]{1,0:T(8,128)(2,1)S(1)} %shard_map.103.refs_2_), channel_id=1, source_target_pairs={{0,8},{1,17},{2,10},{3,19},{4,12},{5,21},{6,14},{7,23},{8,0},{9,25... | collective-permute-start | bytes 1277960 | tf_op jit(solution)/shard_map/ppermute | solution.py:304
  68.7 17.4 %collective-permute-start.10 = (bf16[64,3328]{1,0:T(8,128)(2,1)S(1)}, bf16[64,3328]{1,0:T(8,128)(2,1)S(1)}, u32[]{:S(2)}, u32[]{:S(2)}) collective-permute-start(bf16[64,3328]{1,0:T(8,128)(2,1)S(1)} %get-tuple-element.31), channel_id=1, source_target_pairs={{0,16},{1,9},{2,18},{3,11},{4,20},{5,13},{6,22},{7,15},{8,24},{9,1... | collective-permute-start | bytes 1277960 | tf_op jit(solution)/shard_map/ppermute | solution.py:304
  76.8 19.3 %collective-permute-start.13 = (bf16[64,3328]{1,0:T(8,128)(2,1)S(1)}, bf16[64,3328]{1,0:T(8,128)(2,1)S(1)}, u32[]{:S(2)}, u32[]{:S(2)}) collective-permute-start(bf16[64,3328]{1,0:T(8,128)(2,1)S(1)} %shard_map.106.refs_2_.refs_0_), channel_id=1, source_target_pairs={{0,16},{1,9},{2,18},{3,11},{4,20},{5,13},{6,22},{7,15},{8,24},{9,1... | collective-permute-start | bytes 1277960 | tf_op jit(solution)/shard_map/ppermute | solution.py:304
  79.9 11.1 %collective-permute-start.8 = (bf16[64,1664]{1,0:T(8,128)(2,1)S(1)}, bf16[64,1664]{1,0:T(8,128)(2,1)S(1)}, u32[]{:S(2)}, u32[]{:S(2)}) collective-permute-start(bf16[64,1664]{1,0:T(8,128)(2,1)S(1)} %shard_map.104.refs_3_.refs_0_), channel_id=1, source_target_pairs={{0,8},{1,17},{2,10},{3,19},{4,12},{5,21},{6,14},{7,23},{8,0},{9,25... | collective-permute-start | bytes 638984 | tf_op jit(solution)/shard_map/ppermute | solution.py:304
  86.8 15.4 %collective-permute-start.12 = (bf16[64,1664]{1,0:T(8,128)(2,1)S(1)}, bf16[64,1664]{1,0:T(8,128)(2,1)S(1)}, u32[]{:S(2)}, u32[]{:S(2)}) collective-permute-start(bf16[64,1664]{1,0:T(8,128)(2,1)S(1)} %shard_map.107.refs_2_.refs_0_), channel_id=1, source_target_pairs={{0,16},{1,9},{2,18},{3,11},{4,20},{5,13},{6,22},{7,15},{8,24},{9,1... | collective-permute-start | bytes 638984 | tf_op jit(solution)/shard_map/ppermute | solution.py:304
  102.8 15.8 %collective-permute-start.14 = (bf16[128,1664]{1,0:T(8,128)(2,1)S(1)}, bf16[128,1664]{1,0:T(8,128)(2,1)S(1)}, u32[]{:S(2)}, u32[]{:S(2)}) collective-permute-start(bf16[128,1664]{1,0:T(8,128)(2,1)S(1)} %shard_map.110.refs_1_), channel_id=1, source_target_pairs={{0,8},{1,17},{2,10},{3,19},{4,12},{5,21},{6,14},{7,23},{8,0},{9,25... | collective-permute-start | bytes 1277960 | tf_op jit(solution)/shard_map/ppermute | solution.py:304
  106.2 12.5 %collective-permute-start.15 = (bf16[64,1664]{1,0:T(8,128)(2,1)S(1)}, bf16[64,1664]{1,0:T(8,128)(2,1)S(1)}, u32[]{:S(2)}, u32[]{:S(2)}) collective-permute-start(bf16[64,1664]{1,0:T(8,128)(2,1)S(1)} %shard_map.109.refs_2_.refs_3_), channel_id=1, source_target_pairs={{0,8},{1,17},{2,10},{3,19},{4,12},{5,21},{6,14},{7,23},{8,0},{9,25... | collective-permute-start | bytes 638984 | tf_op jit(solution)/shard_map/ppermute | solution.py:304
  124.2 12.6 %collective-permute-start.21 = (bf16[256,2048]{1,0:T(8,128)(2,1)S(1)}, bf16[256,2048]{1,0:T(8,128)(2,1)S(1)}, u32[]{:S(2)}, u32[]{:S(2)}) collective-permute-start(bf16[256,2048]{1,0:T(8,128)(2,1)S(1)} %shard_map.118), channel_id=1, source_target_pairs={{0,1},{1,0},{2,3},{3,2},{4,5},{5,4},{6,7},{7,6},{8,9},{9,8},{10,11... | collective-permute-start | bytes 3145736 | tf_op jit(solution)/shard_map/ppermute | solution.py:304
  140.3 14.8 %collective-permute-start.17 = (bf16[128,2048]{1,0:T(8,128)(2,1)S(1)}, bf16[128,2048]{1,0:T(8,128)(2,1)S(1)}, u32[]{:S(2)}, u32[]{:S(2)}) collective-permute-start(bf16[128,2048]{1,0:T(8,128)(2,1)S(1)} %get-tuple-element.33), channel_id=1, source_target_pairs={{0,2},{1,5},{2,0},{3,7},{4,6},{5,1},{6,4},{7,3},{8,10},{9,13},{10,... | collective-permute-start | bytes 1572872 | tf_op jit(solution)/shard_map/ppermute | solution.py:304
  188.2 9.8 %collective-permute-start.28 = (f32[256,128]{1,0:T(8,128)S(1)}, f32[256,128]{1,0:T(8,128)S(1)}, u32[]{:S(2)}, u32[]{:S(2)}) collective-permute-start(f32[256,128]{1,0:T(8,128)S(1)} %shard_map.125.after_ref), channel_id=1, source_target_pairs={{0,8},{1,17},{2,10},{3,19},{4,12},{5,21},{6,14},{7,23},{8,0},{9,25... | collective-permute-start | bytes 393224 | tf_op jit(solution)/shard_map/ppermute | solution.py:304
  197.5 14.9 %collective-permute-start.29 = (bf16[256,1024]{1,0:T(8,128)(2,1)S(1)}, bf16[256,1024]{1,0:T(8,128)(2,1)S(1)}, u32[]{:S(2)}, u32[]{:S(2)}) collective-permute-start(bf16[256,1024]{1,0:T(8,128)(2,1)S(1)} %shard_map.127.refs_2_), channel_id=1, source_target_pairs={{0,8},{1,17},{2,10},{3,19},{4,12},{5,21},{6,14},{7,23},{8,0},{9,25... | collective-permute-start | bytes 1572872 | tf_op jit(solution)/shard_map/ppermute | solution.py:304
  198.6 12.9 %collective-permute-start.30 = (f32[128,128]{1,0:T(8,128)S(1)}, f32[128,128]{1,0:T(8,128)S(1)}, u32[]{:S(2)}, u32[]{:S(2)}) collective-permute-start(f32[128,128]{1,0:T(8,128)S(1)} %get-tuple-element.45), channel_id=1, source_target_pairs={{0,16},{1,9},{2,18},{3,11},{4,20},{5,13},{6,22},{7,15},{8,24},{9,1... | collective-permute-start | bytes 196616 | tf_op jit(solution)/shard_map/ppermute | solution.py:304
  209.0 16.9 %collective-permute-start.31 = (bf16[256,1024]{1,0:T(8,128)(2,1)S(1)}, bf16[256,1024]{1,0:T(8,128)(2,1)S(1)}, u32[]{:S(2)}, u32[]{:S(2)}) collective-permute-start(bf16[256,1024]{1,0:T(8,128)(2,1)S(1)} %shard_map.130.refs_2_), channel_id=1, source_target_pairs={{0,8},{1,17},{2,10},{3,19},{4,12},{5,21},{6,14},{7,23},{8,0},{9,25... | collective-permute-start | bytes 1572872 | tf_op jit(solution)/shard_map/ppermute | solution.py:304
  220.8 19.4 %collective-permute-start.33 = (bf16[256,1024]{1,0:T(8,128)(2,1)S(1)}, bf16[256,1024]{1,0:T(8,128)(2,1)S(1)}, u32[]{:S(2)}, u32[]{:S(2)}) collective-permute-start(bf16[256,1024]{1,0:T(8,128)(2,1)S(1)} %shard_map.134.refs_2_), channel_id=1, source_target_pairs={{0,8},{1,17},{2,10},{3,19},{4,12},{5,21},{6,14},{7,23},{8,0},{9,25... | collective-permute-start | bytes 1572872 | tf_op jit(solution)/shard_map/ppermute | solution.py:304
  234.4 29.4 %collective-permute-start.32 = (bf16[256,1024]{1,0:T(8,128)(2,1)S(1)}, bf16[256,1024]{1,0:T(8,128)(2,1)S(1)}, u32[]{:S(2)}, u32[]{:S(2)}) collective-permute-start(bf16[256,1024]{1,0:T(8,128)(2,1)S(1)} %shard_map.137.refs_2_), channel_id=1, source_target_pairs={{0,8},{1,17},{2,10},{3,19},{4,12},{5,21},{6,14},{7,23},{8,0},{9,25... | collective-permute-start | bytes 1572872 | tf_op jit(solution)/shard_map/ppermute | solution.py:304
  234.5 30.3 %collective-permute-start.35 = (bf16[128,1024]{1,0:T(8,128)(2,1)S(1)}, bf16[128,1024]{1,0:T(8,128)(2,1)S(1)}, u32[]{:S(2)}, u32[]{:S(2)}) collective-permute-start(bf16[128,1024]{1,0:T(8,128)(2,1)S(1)} %get-tuple-element.51), channel_id=1, source_target_pairs={{0,16},{1,9},{2,18},{3,11},{4,20},{5,13},{6,22},{7,15},{8,24},{9,1... | collective-permute-start | bytes 786440 | tf_op jit(solution)/shard_map/ppermute | solution.py:304
  236.8 28.0 %collective-permute-start.36 = (bf16[128,1024]{1,0:T(8,128)(2,1)S(1)}, bf16[128,1024]{1,0:T(8,128)(2,1)S(1)}, u32[]{:S(2)}, u32[]{:S(2)}) collective-permute-start(bf16[128,1024]{1,0:T(8,128)(2,1)S(1)} %get-tuple-element.52), channel_id=1, source_target_pairs={{0,16},{1,9},{2,18},{3,11},{4,20},{5,13},{6,22},{7,15},{8,24},{9,1... | collective-permute-start | bytes 786440 | tf_op jit(solution)/shard_map/ppermute | solution.py:304
  240.9 25.5 %collective-permute-start.37 = (bf16[128,1024]{1,0:T(8,128)(2,1)S(1)}, bf16[128,1024]{1,0:T(8,128)(2,1)S(1)}, u32[]{:S(2)}, u32[]{:S(2)}) collective-permute-start(bf16[128,1024]{1,0:T(8,128)(2,1)S(1)} %get-tuple-element.53), channel_id=1, source_target_pairs={{0,16},{1,9},{2,18},{3,11},{4,20},{5,13},{6,22},{7,15},{8,24},{9,1... | collective-permute-start | bytes 786440 | tf_op jit(solution)/shard_map/ppermute | solution.py:304
  (29 other events, 790.6 us)
where the time goes:
time: 294 us; the launch traced here: 293 us
  waiting for transfers between devices  131 us (45%)
  matrix products  67.4 us (23%)
  starting transfers between devices  49.5 us (17%)
  Pallas kernels  33.1 us (11%)
  blocking collectives  7.92 us (3%)
    ppermute x40, waiting for transfers between devices, swapper(): return lambda array: lax.ppermute(array, ('dm', 'hv'), pairs)  131 us
    ppermute x40, starting transfers between devices, swapper(): return lambda array: lax.ppermute(array, ('dm', 'hv'), pairs)  49.5 us
    pallas_call x43, Pallas kernels, run(): pl.pallas_call(kernel, out_shape=[jax.ShapeDtypeStruct(*out) for out in o...  33.1 us
    dot_general x6, matrix products, sums(): jnp.dot(piece, weight, preferred_element_type=F32).astype(BF16)  29.6 us
    dot_general x4, matrix products, on_blocks(): jnp.dot(left, unembed[:, at:at + VOCAB_TILE], preferred_element_type=F32)  28.5 us
    dot_general x2, matrix products, on_blocks(): jnp.dot(hidden, down_weight[:, at:at + width], preferred_element_type=F32)  8.53 us
    all_gather x1, blocking collectives, on_blocks(): stats = lax.all_gather(stats.reshape(4, 8, chip_rows), 'hv', axis=0)  7.92 us
  transfers between devices with their start and end apart: 40, of which 26 were waited for; matrix products, arithmetic and copies ran while one was open for 21% of the time, Pallas kernels for 9%

commit v1 on v0

--- a/solution.py
+++ b/solution.py
@@ -116,18 +116,18 @@
 
 
 def join_below(scalars, above, pairs):
-    rows = above.shape[0] + sum(2 * own.shape[0] for own, _ in pairs)
+    rows = above.shape[0] + sum(2 * own.shape[0] for _, own, _ in pairs)
 
     def body(scalars, above_ref, *refs):
         refs[-1][pl.ds(0, above.shape[0]), :] = above_ref[...]
-        which, at = scalars[DM_FIRST], above.shape[0]
-        for i, (own, _) in enumerate(pairs):
-            size = own.shape[0]
+        at = above.shape[0]
+        for i, (bit, own, _) in enumerate(pairs):
+            which, size = scalars[bit], own.shape[0]
             for place, ref in ((which, refs[2 * i]), (1 - which, refs[2 * i + 1])):
                 refs[-1][pl.ds(pl.multiple_of(at + place * size, 16), size), :] = ref[...]
             at += 2 * size
 
-    arrays = [above, *[array for pair in pairs for array in pair]]
+    arrays = [above, *[array for _, *pair in pairs for array in pair]]
     return run(scalars, body, [((rows, above.shape[1]), above.dtype)], arrays)[0]
 
 
@@ -266,8 +266,8 @@
     def body(scalars, *refs):
         scale_ref, gold_ref, *before_refs, out = refs[2 * many :]
         blocks = []
-        for at in range(0, rows, 16):
-            block = pl.ds(at, 16)
+        for at in range(0, rows, 32):
+            block = pl.ds(at, 32)
             start, chunks = first, []
             for kept, got in zip(refs[:many], refs[many : 2 * many]):
                 logits = (kept[block, :].astype(F32) + got[block, :].astype(F32)) * scale_ref[block, :1]
@@ -285,7 +285,7 @@
             for ref in before_refs:
                 total += ref[block, 1:2] * jnp.exp(ref[block, 0:1] - top)
                 picked += ref[block, 2:3]
-            lane = lax.broadcasted_iota(jnp.int32, (16, 128), 1)
+            lane = lax.broadcasted_iota(jnp.int32, (32, 128), 1)
             blocks.append(jnp.where(lane == 0, top, jnp.where(lane == 1, total, picked)))
         blocks = jnp.concatenate(blocks)
         out[...] = blocks if before is None else blocks.T[:8]
@@ -319,9 +319,9 @@
     gain = norm_gain[None, :]
     chip_rows = 2 * tokens.shape[0]
 
-    def sums(piece):
+    def sums(piece, bit=DM_FIRST):
         both = [jnp.dot(piece, weight, preferred_element_type=F32).astype(BF16) for weight in (gate_weight, up_weight)]
-        return both, pick(scalars, DM_FIRST, both)
+        return both, pick(scalars, bit, both)
 
     tokens = jnp.where(dm < n_dm, tokens, 0)
     from_core, from_x, from_y = cores(tokens), x(tokens), y(tokens)
@@ -329,8 +329,8 @@
     got_0 = z_first(sent_0)
     beside, chosen = stack(scalars, from_x, from_y, sent_0)
     across = xy_last(chosen)
-    both_1, sent_1 = sums(join_chips(scalars, beside, cores(beside)))
-    got_1 = z_first(sent_1)
+    both_1, sent_1 = sums(join_chips(scalars, beside, cores(beside)), DM_LAST)
+    got_1 = z_last(sent_1)
     half_0 = add_half(scalars, DM_FIRST, both_0, got_0, sent_1)
     got_0 = z_last(half_0)
     across = moved(scalars, across, half_0)
@@ -338,17 +338,17 @@
     got_2 = z_first(sent_2)
     own_0 = activate(scalars, half_0, got_0, sent_2)
     got_0 = z_first(own_0)
-    kept_1, sent_1 = add_split(scalars, DM_FIRST, DM_LAST, both_1, got_1, own_0)
-    got_1 = z_last(sent_1)
+    kept_1, sent_1 = add_split(scalars, DM_LAST, DM_FIRST, both_1, got_1, own_0)
+    got_1 = z_first(sent_1)
     half_2 = add_half(scalars, DM_FIRST, both_2, got_2, kept_1)
     got_2 = z_last(half_2)
     own_1 = activate(scalars, kept_1, got_1, half_2)
-    got_1 = z_last(own_1)
+    got_1 = z_first(own_1)
     whole_0 = join(scalars, DM_FIRST, [(own_0, got_0)], own_1)
     own_2 = activate(scalars, half_2, got_2, whole_0)
     got_2 = z_first(own_2)
-    own_1 = join(scalars, DM_LAST, [(own_1, got_1)], own_2)
-    hidden = join_below(scalars, whole_0, [(own_1, z_first(own_1)), (own_2, got_2)])
+    own_1 = join(scalars, DM_FIRST, [(own_1, got_1)], own_2)
+    hidden = join_below(scalars, whole_0, [(DM_LAST, own_1, z_last(own_1)), (DM_FIRST, own_2, got_2)])
     owns, gots = [], []
     width = down_weight.shape[1] // DOWN_CHUNKS
     for at in range(0, down_weight.shape[1], width):

time: 294 us -> 290 us (0.986)
  transfers between devices with their start and end apart: 40 -> 40, of which waited for: 26 -> 25; matrix products, arithmetic and copies ran while one was open for 21% -> 22% of each run, Pallas kernels for 9% -> 8%
where the time goes in v1:
time: 290 us; the launch traced here: 289 us
  waiting for transfers between devices  129 us (44%)
  matrix products  67.5 us (23%)
  starting transfers between devices  48.4 us (17%)
  Pallas kernels  31.6 us (11%)
  blocking collectives  8.51 us (3%)
    ppermute x40, waiting for transfers between devices, swapper(): return lambda array: lax.ppermute(array, ('dm', 'hv'), pairs)  129 us
    ppermute x40, starting transfers between devices, swapper(): return lambda array: lax.ppermute(array, ('dm', 'hv'), pairs)  48.4 us
    pallas_call x43, Pallas kernels, run(): pl.pallas_call(kernel, out_shape=[jax.ShapeDtypeStruct(*out) for out in o...  31.6 us
    dot_general x6, matrix products, sums(): jnp.dot(piece, weight, preferred_element_type=F32).astype(BF16)  29.6 us
    dot_general x4, matrix products, on_blocks(): jnp.dot(left, unembed[:, at:at + VOCAB_TILE], preferred_element_type=F32)  28.5 us
    dot_general x2, matrix products, on_blocks(): jnp.dot(hidden, down_weight[:, at:at + width], preferred_element_type=F32)  8.55 us
    all_gather x1, blocking collectives, on_blocks(): stats = lax.all_gather(stats.reshape(4, 8, chip_rows), 'hv', axis=0)  8.51 us
  transfers between devices with their start and end apart: 40, of which 25 were waited for; matrix products, arithmetic and copies ran while one was open for 22% of the time, Pallas kernels for 8%

profile of v1, /device:TPU:0, one launch (start us, length us, event | category | flops | bytes accessed | tf_op | source)
XLA Modules:
  0.0 289.5 jit_solution(13060671050214273317)
XLA Ops:
  7.1 7.1 %convolution_convert_fusion.4.refs_1_ = bf16[128,1664]{1,0:T(8,128)(2,1)S(1)} fusion(bf16[128,4096]{1,0:T(8,128)(2,1)S(1)} %shard_map.95, bf16[4096,1664]{1,0:T(8,128)(2,1)} %param.10), kind=kOutput, calls=%fused_computation.18 | convolution fusion | flops 1745043456 | bytes 15106048 | tf_op jit(solution)/shard_map/dot_general | solution.py:323
  23.5 4.0 %convolution_convert_fusion.refs_1_ = bf16[256,1664]{1,0:T(8,128)(2,1)S(1)} fusion(bf16[256,4096]{1,0:T(8,128)(2,1)S(1)} %shard_map.98, bf16[4096,1664]{1,0:T(8,128)(2,1)S(1)} %bitcast.46), kind=kOutput, calls=%fused_computation.14 | convolution fusion | flops 3490086912 | bytes 16580608 | tf_op jit(solution)/shard_map/dot_general | solution.py:323
  27.4 7.3 %convolution_convert_fusion.1.refs_0_ = bf16[256,1664]{1,0:T(8,128)(2,1)S(1)} fusion(bf16[256,4096]{1,0:T(8,128)(2,1)S(1)} %shard_map.98, bf16[4096,1664]{1,0:T(8,128)(2,1)} %param.9), kind=kOutput, calls=%fused_computation.15 | convolution fusion | flops 3490086912 | bytes 16580608 | tf_op jit(solution)/shard_map/dot_general | solution.py:323
  42.5 7.1 %convolution_convert_fusion.3.refs_0_ = bf16[128,1664]{1,0:T(8,128)(2,1)S(1)} fusion(bf16[128,4096]{1,0:T(8,128)(2,1)S(1)} %shard_map.102, bf16[4096,1664]{1,0:T(8,128)(2,1)} %param.9), kind=kOutput, calls=%fused_computation.17 | convolution fusion | flops 1745043456 | bytes 15106048 | tf_op jit(solution)/shard_map/dot_general | solution.py:323
  52.4 25.1 %collective-permute-done.9.refs_2_ = bf16[128,3328]{1,0:T(8,128)(2,1)S(1)} collective-permute-done((bf16[128,3328]{1,0:T(8,128)(2,1)S(1)}, bf16[128,3328]{1,0:T(8,128)(2,1)S(1)}, u32[]{:S(2)}, u32[]{:S(2)}) %collective-permute-start.9) | collective-permute-done | bytes 852000 | tf_op jit(solution)/shard_map/ppermute | solution.py:304
  78.2 7.4 %collective-permute-start.10 = (bf16[64,3328]{1,0:T(8,128)(2,1)S(1)}, bf16[64,3328]{1,0:T(8,128)(2,1)S(1)}, u32[]{:S(2)}, u32[]{:S(2)}) collective-permute-start(bf16[64,3328]{1,0:T(8,128)(2,1)S(1)} %get-tuple-element.31), channel_id=1, source_target_pairs={{0,8},{1,17},{2,10},{3,19},{4,12},{5,21},{6,14},{7,23},{8,0},{9,25... | collective-permute-start | bytes 1277960 | tf_op jit(solution)/shard_map/ppermute | solution.py:304
  89.8 8.7 %collective-permute-done.10.refs_1_ = bf16[64,3328]{1,0:T(8,128)(2,1)S(1)} collective-permute-done((bf16[64,3328]{1,0:T(8,128)(2,1)S(1)}, bf16[64,3328]{1,0:T(8,128)(2,1)S(1)}, u32[]{:S(2)}, u32[]{:S(2)}) %collective-permute-start.10) | collective-permute-done | bytes 426016 | tf_op jit(solution)/shard_map/ppermute | solution.py:304
  102.4 3.7 %collective-permute-done.13.refs_1_ = bf16[64,3328]{1,0:T(8,128)(2,1)S(1)} collective-permute-done((bf16[64,3328]{1,0:T(8,128)(2,1)S(1)}, bf16[64,3328]{1,0:T(8,128)(2,1)S(1)}, u32[]{:S(2)}, u32[]{:S(2)}) %collective-permute-start.13) | collective-permute-done | bytes 426016 | tf_op jit(solution)/shard_map/ppermute | solution.py:304
  112.0 7.5 %collective-permute-done.15.refs_4_ = bf16[64,1664]{1,0:T(8,128)(2,1)S(1)} collective-permute-done((bf16[64,1664]{1,0:T(8,128)(2,1)S(1)}, bf16[64,1664]{1,0:T(8,128)(2,1)S(1)}, u32[]{:S(2)}, u32[]{:S(2)}) %collective-permute-start.15) | collective-permute-done | bytes 213024 | tf_op jit(solution)/shard_map/ppermute | solution.py:304
  119.6 5.1 %collective-permute-done.14.refs_2_ = bf16[128,1664]{1,0:T(8,128)(2,1)S(1)} collective-permute-done((bf16[128,1664]{1,0:T(8,128)(2,1)S(1)}, bf16[128,1664]{1,0:T(8,128)(2,1)S(1)}, u32[]{:S(2)}, u32[]{:S(2)}) %collective-permute-start.14) | collective-permute-done | bytes 426016 | tf_op jit(solution)/shard_map/ppermute | solution.py:304
  125.4 4.2 %fusion.15.refs_0_ = bf16[512,2048]{1,0:T(8,128)(2,1)S(1)} fusion(bf16[512,1664]{1,0:T(8,128)(2,1)S(1)} %shard_map.111, bf16[1664,4096]{1,0:T(8,128)(2,1)S(1)} %bitcast.56), kind=kOutput, calls=%fused_computation.13 | convolution fusion | flops 3490709504 | bytes 10616832 | tf_op jit(solution)/shard_map/dot_general | solution.py:355
  130.2 4.4 %fusion.12.refs_0_ = bf16[512,2048]{1,0:T(8,128)(2,1)S(1)} fusion(bf16[512,1664]{1,0:T(8,128)(2,1)S(1)} %shard_map.111, bf16[1664,4096]{1,0:T(8,128)(2,1)S(1)} %bitcast.56), kind=kOutput, calls=%fused_computation.12 | convolution fusion | flops 3490709504 | bytes 10616832 | tf_op jit(solution)/shard_map/dot_general | solution.py:355
  139.6 6.3 %collective-permute-done.22.refs_1_ = bf16[128,2048]{1,0:T(8,128)(2,1)S(1)} collective-permute-done((bf16[128,2048]{1,0:T(8,128)(2,1)S(1)}, bf16[128,2048]{1,0:T(8,128)(2,1)S(1)}, u32[]{:S(2)}, u32[]{:S(2)}) %collective-permute-start.22) | collective-permute-done | bytes 524320 | tf_op jit(solution)/shard_map/ppermute | solution.py:304
  147.9 6.4 %collective-permute-done.17.refs_1_ = bf16[128,2048]{1,0:T(8,128)(2,1)S(1)} collective-permute-done((bf16[128,2048]{1,0:T(8,128)(2,1)S(1)}, bf16[128,2048]{1,0:T(8,128)(2,1)S(1)}, u32[]{:S(2)}, u32[]{:S(2)}) %collective-permute-start.17) | collective-permute-done | bytes 524320 | tf_op jit(solution)/shard_map/ppermute | solution.py:304
  165.9 5.5 %collective-permute-done.19.refs_1_ = bf16[64,2048]{1,0:T(8,128)(2,1)S(1)} collective-permute-done((bf16[64,2048]{1,0:T(8,128)(2,1)S(1)}, bf16[64,2048]{1,0:T(8,128)(2,1)S(1)}, u32[]{:S(2)}, u32[]{:S(2)}) %collective-permute-start.19) | collective-permute-done | bytes 262176 | tf_op jit(solution)/shard_map/ppermute | solution.py:304
  175.2 6.5 %collective-permute-done.20.refs_1_ = bf16[128,2048]{1,0:T(8,128)(2,1)S(1)} collective-permute-done((bf16[128,2048]{1,0:T(8,128)(2,1)S(1)}, bf16[128,2048]{1,0:T(8,128)(2,1)S(1)}, u32[]{:S(2)}, u32[]{:S(2)}) %collective-permute-start.20) | collective-permute-done | bytes 524320 | tf_op jit(solution)/shard_map/ppermute | solution.py:304
  187.6 7.1 %fusion.21.refs_0_ = bf16[512,1024]{1,0:T(8,128)(2,1)S(1)} fusion(bf16[512,4096]{1,0:T(8,128)(2,1)S(1)} %shard_map.126.array_ref, bf16[4096,4008]{0,1:T(8,128)(2,1)} %param.13), kind=kOutput, calls=%fused_computation.21 | convolution fusion | flops 4295491584 | bytes 13631488 | tf_op jit(solution)/shard_map/dot_general | solution.py:369
  198.0 7.1 %fusion.24.refs_0_ = bf16[512,1024]{1,0:T(8,128)(2,1)S(1)} fusion(bf16[512,4096]{1,0:T(8,128)(2,1)S(1)} %shard_map.129.array_ref, bf16[4096,4008]{0,1:T(8,128)(2,1)} %param.13), kind=kOutput, calls=%fused_computation.22 | convolution fusion | flops 4295491584 | bytes 13631488 | tf_op jit(solution)/shard_map/dot_general | solution.py:369
  213.3 7.1 %fusion.27.refs_0_ = bf16[512,1024]{1,0:T(8,128)(2,1)S(1)} fusion(bf16[512,4096]{1,0:T(8,128)(2,1)S(1)} %shard_map.133.array_ref, bf16[4096,4008]{0,1:T(8,128)(2,1)} %param.13), kind=kOutput, calls=%fused_computation.23 | convolution fusion | flops 4295491584 | bytes 13631488 | tf_op jit(solution)/shard_map/dot_general | solution.py:369
  223.4 7.2 %fusion.18.refs_0_ = bf16[512,936]{1,0:T(8,128)(2,1)S(1)} fusion(bf16[512,4096]{1,0:T(8,128)(2,1)S(1)} %shard_map.136, bf16[4096,4008]{0,1:T(8,128)(2,1)} %param.13), kind=kOutput, calls=%fused_computation.20 | convolution fusion | flops 3926347776 | bytes 12820480 | tf_op jit(solution)/shard_map/dot_general | solution.py:369
  238.4 20.4 %collective-permute-done.32.refs_1_ = bf16[256,1024]{1,0:T(8,128)(2,1)S(1)} collective-permute-done((bf16[256,1024]{1,0:T(8,128)(2,1)S(1)}, bf16[256,1024]{1,0:T(8,128)(2,1)S(1)}, u32[]{:S(2)}, u32[]{:S(2)}) %collective-permute-start.32) | collective-permute-done | bytes 524320 | tf_op jit(solution)/shard_map/ppermute | solution.py:304
  263.7 6.5 %collective-permute-done.34.refs_1_ = bf16[128,1024]{1,0:T(8,128)(2,1)S(1)} collective-permute-done((bf16[128,1024]{1,0:T(8,128)(2,1)S(1)}, bf16[128,1024]{1,0:T(8,128)(2,1)S(1)}, u32[]{:S(2)}, u32[]{:S(2)}) %collective-permute-start.34) | collective-permute-done | bytes 262176 | tf_op jit(solution)/shard_map/ppermute | solution.py:304
  272.6 3.8 %collective-permute-done.38 = f32[1,8,128]{2,1,0:T(8,128)S(1)} collective-permute-done((f32[1,8,128]{2,1,0:T(8,128)S(1)}, f32[1,8,128]{2,1,0:T(8,128)S(1)}, u32[]{:S(2)}, u32[]{:S(2)}) %collective-permute-start.38) | collective-permute-done | bytes 4128 | tf_op jit(solution)/shard_map/ppermute | solution.py:304
  280.1 8.5 %all_gather.3 = f32[8,4,8,128]{3,2,1,0:T(8,128)S(1)} all-gather(f32[1,4,8,128]{3,2,1,0:T(8,128)S(1)} %bitcast.49), channel_id=1, replica_groups=mesh['dm'=4,'hv'=8] {'hv'}, dimensions={0}, use_global_device_ids=true | all-gather | bytes 147456 | tf_op jit(solution)/shard_map/all_gather | solution.py:395
  (163 shorter events, 104.3 us)
Async XLA Ops:
  2.3 16.2 %collective-permute-start.2 = (bf16[64,4096]{1,0:T(8,128)(2,1)S(1)}, bf16[64,4096]{1,0:T(8,128)(2,1)S(1)}, u32[]{:S(2)}, u32[]{:S(2)}) collective-permute-start(bf16[64,4096]{1,0:T(8,128)(2,1)S(1)} %broadcast_select_fusion.refs_0_), channel_id=1, source_target_pairs={{0,2},{1,3},{2,0},{3,1},{4,6},{5,7},{6,4},{7,5},{8,10},{9,11},{10,... | collective-permute-start | bytes 1572872 | tf_op jit(solution)/shard_map/ppermute | solution.py:304
  4.8 14.0 %collective-permute-start.3 = (bf16[64,4096]{1,0:T(8,128)(2,1)S(1)}, bf16[64,4096]{1,0:T(8,128)(2,1)S(1)}, u32[]{:S(2)}, u32[]{:S(2)}) collective-permute-start(bf16[64,4096]{1,0:T(8,128)(2,1)S(1)} %broadcast_select_fusion.refs_0_), channel_id=1, source_target_pairs={{0,4},{1,5},{2,6},{3,7},{4,0},{5,1},{6,2},{7,3},{8,12},{9,13},{10,... | collective-permute-start | bytes 1572872 | tf_op jit(solution)/shard_map/ppermute | solution.py:304
  19.6 15.8 %collective-permute-start.1 = (bf16[64,3328]{1,0:T(8,128)(2,1)S(1)}, bf16[64,3328]{1,0:T(8,128)(2,1)S(1)}, u32[]{:S(2)}, u32[]{:S(2)}) collective-permute-start(bf16[64,3328]{1,0:T(8,128)(2,1)S(1)} %shard_map.96.refs_2_), channel_id=1, source_target_pairs={{0,8},{1,17},{2,10},{3,19},{4,12},{5,21},{6,14},{7,23},{8,0},{9,25... | collective-permute-start | bytes 1277960 | tf_op jit(solution)/shard_map/ppermute | solution.py:304
  21.2 14.9 %collective-permute-start.6 = (bf16[64,4096]{1,0:T(8,128)(2,1)S(1)}, bf16[64,4096]{1,0:T(8,128)(2,1)S(1)}, u32[]{:S(2)}, u32[]{:S(2)}) collective-permute-start(bf16[64,4096]{1,0:T(8,128)(2,1)S(1)} %get-tuple-element.29), channel_id=1, source_target_pairs={{0,4},{1,3},{2,6},{3,1},{4,0},{5,7},{6,2},{7,5},{8,12},{9,11},{10,... | collective-permute-start | bytes 1572872 | tf_op jit(solution)/shard_map/ppermute | solution.py:304
  36.7 14.9 %collective-permute-start.5 = (bf16[64,3328]{1,0:T(8,128)(2,1)S(1)}, bf16[64,3328]{1,0:T(8,128)(2,1)S(1)}, u32[]{:S(2)}, u32[]{:S(2)}) collective-permute-start(bf16[64,3328]{1,0:T(8,128)(2,1)S(1)} %shard_map.100.refs_1_.refs_0_), channel_id=1, source_target_pairs={{0,16},{1,9},{2,18},{3,11},{4,20},{5,13},{6,22},{7,15},{8,24},{9,1... | collective-permute-start | bytes 1277960 | tf_op jit(solution)/shard_map/ppermute | solution.py:304
  39.4 38.0 %collective-permute-start.9 = (bf16[128,3328]{1,0:T(8,128)(2,1)S(1)}, bf16[128,3328]{1,0:T(8,128)(2,1)S(1)}, u32[]{:S(2)}, u32[]{:S(2)}) collective-permute-start(bf16[128,3328]{1,0:T(8,128)(2,1)S(1)} %shard_map.99.refs_3_), channel_id=1, source_target_pairs={{0,16},{1,9},{2,18},{3,11},{4,20},{5,13},{6,22},{7,15},{8,24},{9,1... | collective-permute-start | bytes 2555912 | tf_op jit(solution)/shard_map/ppermute | solution.py:304
  50.2 35.4 %collective-permute-start.11 = (bf16[64,3328]{1,0:T(8,128)(2,1)S(1)}, bf16[64,3328]{1,0:T(8,128)(2,1)S(1)}, u32[]{:S(2)}, u32[]{:S(2)}) collective-permute-start(bf16[64,3328]{1,0:T(8,128)(2,1)S(1)} %shard_map.103.refs_2_), channel_id=1, source_target_pairs={{0,8},{1,17},{2,10},{3,19},{4,12},{5,21},{6,14},{7,23},{8,0},{9,25... | collective-permute-start | bytes 1277960 | tf_op jit(solution)/shard_map/ppermute | solution.py:304
  78.2 20.2 %collective-permute-start.10 = (bf16[64,3328]{1,0:T(8,128)(2,1)S(1)}, bf16[64,3328]{1,0:T(8,128)(2,1)S(1)}, u32[]{:S(2)}, u32[]{:S(2)}) collective-permute-start(bf16[64,3328]{1,0:T(8,128)(2,1)S(1)} %get-tuple-element.31), channel_id=1, source_target_pairs={{0,8},{1,17},{2,10},{3,19},{4,12},{5,21},{6,14},{7,23},{8,0},{9,25... | collective-permute-start | bytes 1277960 | tf_op jit(solution)/shard_map/ppermute | solution.py:304
  86.2 19.8 %collective-permute-start.13 = (bf16[64,3328]{1,0:T(8,128)(2,1)S(1)}, bf16[64,3328]{1,0:T(8,128)(2,1)S(1)}, u32[]{:S(2)}, u32[]{:S(2)}) collective-permute-start(bf16[64,3328]{1,0:T(8,128)(2,1)S(1)} %shard_map.106.refs_2_.refs_0_), channel_id=1, source_target_pairs={{0,16},{1,9},{2,18},{3,11},{4,20},{5,13},{6,22},{7,15},{8,24},{9,1... | collective-permute-start | bytes 1277960 | tf_op jit(solution)/shard_map/ppermute | solution.py:304
  89.7 12.1 %collective-permute-start.8 = (bf16[64,1664]{1,0:T(8,128)(2,1)S(1)}, bf16[64,1664]{1,0:T(8,128)(2,1)S(1)}, u32[]{:S(2)}, u32[]{:S(2)}) collective-permute-start(bf16[64,1664]{1,0:T(8,128)(2,1)S(1)} %shard_map.104.refs_3_.refs_0_), channel_id=1, source_target_pairs={{0,8},{1,17},{2,10},{3,19},{4,12},{5,21},{6,14},{7,23},{8,0},{9,25... | collective-permute-start | bytes 638984 | tf_op jit(solution)/shard_map/ppermute | solution.py:304
  109.0 15.6 %collective-permute-start.14 = (bf16[128,1664]{1,0:T(8,128)(2,1)S(1)}, bf16[128,1664]{1,0:T(8,128)(2,1)S(1)}, u32[]{:S(2)}, u32[]{:S(2)}) collective-permute-start(bf16[128,1664]{1,0:T(8,128)(2,1)S(1)} %shard_map.110.refs_1_), channel_id=1, source_target_pairs={{0,16},{1,9},{2,18},{3,11},{4,20},{5,13},{6,22},{7,15},{8,24},{9,1... | collective-permute-start | bytes 1277960 | tf_op jit(solution)/shard_map/ppermute | solution.py:304
  109.6 10.0 %collective-permute-start.15 = (bf16[64,1664]{1,0:T(8,128)(2,1)S(1)}, bf16[64,1664]{1,0:T(8,128)(2,1)S(1)}, u32[]{:S(2)}, u32[]{:S(2)}) collective-permute-start(bf16[64,1664]{1,0:T(8,128)(2,1)S(1)} %shard_map.109.refs_2_.refs_3_), channel_id=1, source_target_pairs={{0,8},{1,17},{2,10},{3,19},{4,12},{5,21},{6,14},{7,23},{8,0},{9,25... | collective-permute-start | bytes 638984 | tf_op jit(solution)/shard_map/ppermute | solution.py:304
  138.9 15.4 %collective-permute-start.17 = (bf16[128,2048]{1,0:T(8,128)(2,1)S(1)}, bf16[128,2048]{1,0:T(8,128)(2,1)S(1)}, u32[]{:S(2)}, u32[]{:S(2)}) collective-permute-start(bf16[128,2048]{1,0:T(8,128)(2,1)S(1)} %get-tuple-element.33), channel_id=1, source_target_pairs={{0,2},{1,5},{2,0},{3,7},{4,6},{5,1},{6,4},{7,3},{8,10},{9,13},{10,... | collective-permute-start | bytes 1572872 | tf_op jit(solution)/shard_map/ppermute | solution.py:304
  146.5 9.8 %collective-permute-start.23 = (bf16[64,2048]{1,0:T(8,128)(2,1)S(1)}, bf16[64,2048]{1,0:T(8,128)(2,1)S(1)}, u32[]{:S(2)}, u32[]{:S(2)}) collective-permute-start(bf16[64,2048]{1,0:T(8,128)(2,1)S(1)} %get-tuple-element.40), channel_id=1, source_target_pairs={{0,4},{1,3},{2,6},{3,1},{4,0},{5,7},{6,2},{7,5},{8,12},{9,11},{10,... | collective-permute-start | bytes 786440 | tf_op jit(solution)/shard_map/ppermute | solution.py:304
  187.5 9.8 %collective-permute-start.28 = (f32[256,128]{1,0:T(8,128)S(1)}, f32[256,128]{1,0:T(8,128)S(1)}, u32[]{:S(2)}, u32[]{:S(2)}) collective-permute-start(f32[256,128]{1,0:T(8,128)S(1)} %shard_map.125.after_ref), channel_id=1, source_target_pairs={{0,8},{1,17},{2,10},{3,19},{4,12},{5,21},{6,14},{7,23},{8,0},{9,25... | collective-permute-start | bytes 393224 | tf_op jit(solution)/shard_map/ppermute | solution.py:304
  195.3 17.4 %collective-permute-start.29 = (bf16[256,1024]{1,0:T(8,128)(2,1)S(1)}, bf16[256,1024]{1,0:T(8,128)(2,1)S(1)}, u32[]{:S(2)}, u32[]{:S(2)}) collective-permute-start(bf16[256,1024]{1,0:T(8,128)(2,1)S(1)} %shard_map.127.refs_2_), channel_id=1, source_target_pairs={{0,8},{1,17},{2,10},{3,19},{4,12},{5,21},{6,14},{7,23},{8,0},{9,25... | collective-permute-start | bytes 1572872 | tf_op jit(solution)/shard_map/ppermute | solution.py:304
  197.9 13.1 %collective-permute-start.30 = (f32[128,128]{1,0:T(8,128)S(1)}, f32[128,128]{1,0:T(8,128)S(1)}, u32[]{:S(2)}, u32[]{:S(2)}) collective-permute-start(f32[128,128]{1,0:T(8,128)S(1)} %get-tuple-element.45), channel_id=1, source_target_pairs={{0,16},{1,9},{2,18},{3,11},{4,20},{5,13},{6,22},{7,15},{8,24},{9,1... | collective-permute-start | bytes 196616 | tf_op jit(solution)/shard_map/ppermute | solution.py:304
  205.7 17.1 %collective-permute-start.31 = (bf16[256,1024]{1,0:T(8,128)(2,1)S(1)}, bf16[256,1024]{1,0:T(8,128)(2,1)S(1)}, u32[]{:S(2)}, u32[]{:S(2)}) collective-permute-start(bf16[256,1024]{1,0:T(8,128)(2,1)S(1)} %shard_map.130.refs_2_), channel_id=1, source_target_pairs={{0,8},{1,17},{2,10},{3,19},{4,12},{5,21},{6,14},{7,23},{8,0},{9,25... | collective-permute-start | bytes 1572872 | tf_op jit(solution)/shard_map/ppermute | solution.py:304
  221.0 15.1 %collective-permute-start.33 = (bf16[256,1024]{1,0:T(8,128)(2,1)S(1)}, bf16[256,1024]{1,0:T(8,128)(2,1)S(1)}, u32[]{:S(2)}, u32[]{:S(2)}) collective-permute-start(bf16[256,1024]{1,0:T(8,128)(2,1)S(1)} %shard_map.134.refs_2_), channel_id=1, source_target_pairs={{0,8},{1,17},{2,10},{3,19},{4,12},{5,21},{6,14},{7,23},{8,0},{9,25... | collective-permute-start | bytes 1572872 | tf_op jit(solution)/shard_map/ppermute | solution.py:304
  231.3 27.5 %collective-permute-start.32 = (bf16[256,1024]{1,0:T(8,128)(2,1)S(1)}, bf16[256,1024]{1,0:T(8,128)(2,1)S(1)}, u32[]{:S(2)}, u32[]{:S(2)}) collective-permute-start(bf16[256,1024]{1,0:T(8,128)(2,1)S(1)} %shard_map.137.refs_2_), channel_id=1, source_target_pairs={{0,8},{1,17},{2,10},{3,19},{4,12},{5,21},{6,14},{7,23},{8,0},{9,25... | collective-permute-start | bytes 1572872 | tf_op jit(solution)/shard_map/ppermute | solution.py:304
  233.2 27.1 %collective-permute-start.35 = (bf16[128,1024]{1,0:T(8,128)(2,1)S(1)}, bf16[128,1024]{1,0:T(8,128)(2,1)S(1)}, u32[]{:S(2)}, u32[]{:S(2)}) collective-permute-start(bf16[128,1024]{1,0:T(8,128)(2,1)S(1)} %get-tuple-element.51), channel_id=1, source_target_pairs={{0,16},{1,9},{2,18},{3,11},{4,20},{5,13},{6,22},{7,15},{8,24},{9,1... | collective-permute-start | bytes 786440 | tf_op jit(solution)/shard_map/ppermute | solution.py:304
  234.1 26.2 %collective-permute-start.36 = (bf16[128,1024]{1,0:T(8,128)(2,1)S(1)}, bf16[128,1024]{1,0:T(8,128)(2,1)S(1)}, u32[]{:S(2)}, u32[]{:S(2)}) collective-permute-start(bf16[128,1024]{1,0:T(8,128)(2,1)S(1)} %get-tuple-element.52), channel_id=1, source_target_pairs={{0,16},{1,9},{2,18},{3,11},{4,20},{5,13},{6,22},{7,15},{8,24},{9,1... | collective-permute-start | bytes 786440 | tf_op jit(solution)/shard_map/ppermute | solution.py:304
  236.8 25.5 %collective-permute-start.37 = (bf16[128,1024]{1,0:T(8,128)(2,1)S(1)}, bf16[128,1024]{1,0:T(8,128)(2,1)S(1)}, u32[]{:S(2)}, u32[]{:S(2)}) collective-permute-start(bf16[128,1024]{1,0:T(8,128)(2,1)S(1)} %get-tuple-element.53), channel_id=1, source_target_pairs={{0,16},{1,9},{2,18},{3,11},{4,20},{5,13},{6,22},{7,15},{8,24},{9,1... | collective-permute-start | bytes 786440 | tf_op jit(solution)/shard_map/ppermute | solution.py:304
  259.5 10.7 %collective-permute-start.34 = (bf16[128,1024]{1,0:T(8,128)(2,1)S(1)}, bf16[128,1024]{1,0:T(8,128)(2,1)S(1)}, u32[]{:S(2)}, u32[]{:S(2)}) collective-permute-start(bf16[128,1024]{1,0:T(8,128)(2,1)S(1)} %get-tuple-element.50), channel_id=1, source_target_pairs={{0,16},{1,9},{2,18},{3,11},{4,20},{5,13},{6,22},{7,15},{8,24},{9,1... | collective-permute-start | bytes 786440 | tf_op jit(solution)/shard_map/ppermute | solution.py:304
  (29 other events, 797.5 us)

commit v2 on v1

--- a/solution.py
+++ b/solution.py
@@ -385,10 +385,12 @@
     columns = unembed.shape[1]
     stats = row_stats(scalars, kepts, gots, scale, gold, 0, columns, None, last)
     stats = row_stats(scalars, [last], [z_last(sent)], scale, gold, VOCAB_TILE * len(kepts), columns, stats)
+    def ordered(bit, own, got):
+        return jnp.concatenate([jnp.where(bit == 0, own, got), jnp.where(bit == 0, got, own)])
+
     stats = stats[None]
-    for bit, swap in ((dm_last, z_last), (dm_first, z_first)):
-        got = swap(stats)
-        stats = jnp.concatenate([jnp.where(bit == 0, stats, got), jnp.where(bit == 0, got, stats)])
+    beside, across, opposite = z_last(stats), z_first(stats), swapper(n_dm, n_hv, True, lambda hv: 3)(stats)
+    stats = ordered(dm_first, ordered(dm_last, stats, beside), ordered(dm_last, across, opposite))
     stats = stats.reshape(2, 2, 8, chip_rows)
     stats = jnp.where(chip & 1 == 0, stats, stats[:, ::-1])
     stats = jnp.where(chip >> 1 == 0, stats, stats[::-1])

time: 290 us -> 290 us (level)
  starting transfers between devices: 48.4 us -> 51.4 us
  waiting for transfers between devices: 129 us -> 126 us
    ppermute x40 -> x41, waiting for transfers between devices: 129 us -> 126 us  [swapper(): return lambda array: lax.ppermute(array, ('dm', 'hv'), pairs)]
    ppermute x40 -> x41, starting transfers between devices: 48.4 us -> 51.4 us  [swapper(): return lambda array: lax.ppermute(array, ('dm', 'hv'), pairs)]
  transfers between devices with their start and end apart: 40 -> 41, of which waited for: 25 -> 24; matrix products, arithmetic and copies ran while one was open for 22% -> 22% of each run, Pallas kernels for 8% -> 8%
where the time goes in v2:
time: 290 us
  waiting for transfers between devices  126 us (43%)
  matrix products  67.8 us (23%)
  starting transfers between devices  51.4 us (18%)
  Pallas kernels  31.6 us (11%)
  blocking collectives  8.78 us (3%)
    ppermute x41, waiting for transfers between devices, swapper(): return lambda array: lax.ppermute(array, ('dm', 'hv'), pairs)  126 us
    ppermute x41, starting transfers between devices, swapper(): return lambda array: lax.ppermute(array, ('dm', 'hv'), pairs)  51.4 us
    pallas_call x43, Pallas kernels, run(): pl.pallas_call(kernel, out_shape=[jax.ShapeDtypeStruct(*out) for out in o...  31.6 us
    dot_general x6, matrix products, sums(): jnp.dot(piece, weight, preferred_element_type=F32).astype(BF16)  30 us
    dot_general x4, matrix products, on_blocks(): jnp.dot(left, unembed[:, at:at + VOCAB_TILE], preferred_element_type=F32)  28.5 us
    all_gather x1, blocking collectives, on_blocks(): stats = lax.all_gather(stats.reshape(4, 8, chip_rows), 'hv', axis=0)  8.78 us
    dot_general x2, matrix products, on_blocks(): jnp.dot(hidden, down_weight[:, at:at + width], preferred_element_type=F32)  8.55 us
  transfers between devices with their start and end apart: 41, of which 24 were waited for; matrix products, arithmetic and copies ran while one was open for 22% of the time, Pallas kernels for 8%

profile of v2, /device:TPU:0, one launch (start us, length us, event | category | flops | bytes accessed | tf_op | source)
XLA Modules:
  0.0 289.9 jit_solution(8461158623467677825)
XLA Ops:
  7.1 7.1 %convolution_convert_fusion.4.refs_1_ = bf16[128,1664]{1,0:T(8,128)(2,1)S(1)} fusion(bf16[128,4096]{1,0:T(8,128)(2,1)S(1)} %shard_map.95, bf16[4096,1664]{1,0:T(8,128)(2,1)} %param.10), kind=kOutput, calls=%fused_computation.18 | convolution fusion | flops 1745043456 | bytes 15106048 | tf_op jit(solution)/shard_map/dot_general | solution.py:323
  23.5 4.0 %convolution_convert_fusion.refs_1_ = bf16[256,1664]{1,0:T(8,128)(2,1)S(1)} fusion(bf16[256,4096]{1,0:T(8,128)(2,1)S(1)} %shard_map.98, bf16[4096,1664]{1,0:T(8,128)(2,1)S(1)} %bitcast.48), kind=kOutput, calls=%fused_computation.14 | convolution fusion | flops 3490086912 | bytes 16580608 | tf_op jit(solution)/shard_map/dot_general | solution.py:323
  27.5 7.4 %convolution_convert_fusion.1.refs_0_ = bf16[256,1664]{1,0:T(8,128)(2,1)S(1)} fusion(bf16[256,4096]{1,0:T(8,128)(2,1)S(1)} %shard_map.98, bf16[4096,1664]{1,0:T(8,128)(2,1)} %param.9), kind=kOutput, calls=%fused_computation.15 | convolution fusion | flops 3490086912 | bytes 16580608 | tf_op jit(solution)/shard_map/dot_general | solution.py:323
  42.7 7.1 %convolution_convert_fusion.3.refs_0_ = bf16[128,1664]{1,0:T(8,128)(2,1)S(1)} fusion(bf16[128,4096]{1,0:T(8,128)(2,1)S(1)} %shard_map.102, bf16[4096,1664]{1,0:T(8,128)(2,1)} %param.9), kind=kOutput, calls=%fused_computation.17 | convolution fusion | flops 1745043456 | bytes 15106048 | tf_op jit(solution)/shard_map/dot_general | solution.py:323
  52.6 24.9 %collective-permute-done.9.refs_2_ = bf16[128,3328]{1,0:T(8,128)(2,1)S(1)} collective-permute-done((bf16[128,3328]{1,0:T(8,128)(2,1)S(1)}, bf16[128,3328]{1,0:T(8,128)(2,1)S(1)}, u32[]{:S(2)}, u32[]{:S(2)}) %collective-permute-start.9) | collective-permute-done | bytes 852000 | tf_op jit(solution)/shard_map/ppermute | solution.py:304
  78.3 7.4 %collective-permute-start.10 = (bf16[64,3328]{1,0:T(8,128)(2,1)S(1)}, bf16[64,3328]{1,0:T(8,128)(2,1)S(1)}, u32[]{:S(2)}, u32[]{:S(2)}) collective-permute-start(bf16[64,3328]{1,0:T(8,128)(2,1)S(1)} %get-tuple-element.31), channel_id=1, source_target_pairs={{0,8},{1,17},{2,10},{3,19},{4,12},{5,21},{6,14},{7,23},{8,0},{9,25... | collective-permute-start | bytes 1277960 | tf_op jit(solution)/shard_map/ppermute | solution.py:304
  89.9 8.7 %collective-permute-done.10.refs_1_ = bf16[64,3328]{1,0:T(8,128)(2,1)S(1)} collective-permute-done((bf16[64,3328]{1,0:T(8,128)(2,1)S(1)}, bf16[64,3328]{1,0:T(8,128)(2,1)S(1)}, u32[]{:S(2)}, u32[]{:S(2)}) %collective-permute-start.10) | collective-permute-done | bytes 426016 | tf_op jit(solution)/shard_map/ppermute | solution.py:304
  102.5 3.7 %collective-permute-done.13.refs_1_ = bf16[64,3328]{1,0:T(8,128)(2,1)S(1)} collective-permute-done((bf16[64,3328]{1,0:T(8,128)(2,1)S(1)}, bf16[64,3328]{1,0:T(8,128)(2,1)S(1)}, u32[]{:S(2)}, u32[]{:S(2)}) %collective-permute-start.13) | collective-permute-done | bytes 426016 | tf_op jit(solution)/shard_map/ppermute | solution.py:304
  112.2 7.6 %collective-permute-done.15.refs_4_ = bf16[64,1664]{1,0:T(8,128)(2,1)S(1)} collective-permute-done((bf16[64,1664]{1,0:T(8,128)(2,1)S(1)}, bf16[64,1664]{1,0:T(8,128)(2,1)S(1)}, u32[]{:S(2)}, u32[]{:S(2)}) %collective-permute-start.15) | collective-permute-done | bytes 213024 | tf_op jit(solution)/shard_map/ppermute | solution.py:304
  119.7 5.0 %collective-permute-done.14.refs_2_ = bf16[128,1664]{1,0:T(8,128)(2,1)S(1)} collective-permute-done((bf16[128,1664]{1,0:T(8,128)(2,1)S(1)}, bf16[128,1664]{1,0:T(8,128)(2,1)S(1)}, u32[]{:S(2)}, u32[]{:S(2)}) %collective-permute-start.14) | collective-permute-done | bytes 426016 | tf_op jit(solution)/shard_map/ppermute | solution.py:304
  125.5 4.2 %fusion.15.refs_0_ = bf16[512,2048]{1,0:T(8,128)(2,1)S(1)} fusion(bf16[512,1664]{1,0:T(8,128)(2,1)S(1)} %shard_map.111, bf16[1664,4096]{1,0:T(8,128)(2,1)S(1)} %bitcast.58), kind=kOutput, calls=%fused_computation.13 | convolution fusion | flops 3490709504 | bytes 10616832 | tf_op jit(solution)/shard_map/dot_general | solution.py:355
  130.4 4.4 %fusion.12.refs_0_ = bf16[512,2048]{1,0:T(8,128)(2,1)S(1)} fusion(bf16[512,1664]{1,0:T(8,128)(2,1)S(1)} %shard_map.111, bf16[1664,4096]{1,0:T(8,128)(2,1)S(1)} %bitcast.58), kind=kOutput, calls=%fused_computation.12 | convolution fusion | flops 3490709504 | bytes 10616832 | tf_op jit(solution)/shard_map/dot_general | solution.py:355
  139.7 6.3 %collective-permute-done.22.refs_1_ = bf16[128,2048]{1,0:T(8,128)(2,1)S(1)} collective-permute-done((bf16[128,2048]{1,0:T(8,128)(2,1)S(1)}, bf16[128,2048]{1,0:T(8,128)(2,1)S(1)}, u32[]{:S(2)}, u32[]{:S(2)}) %collective-permute-start.22) | collective-permute-done | bytes 524320 | tf_op jit(solution)/shard_map/ppermute | solution.py:304
  148.1 6.3 %collective-permute-done.17.refs_1_ = bf16[128,2048]{1,0:T(8,128)(2,1)S(1)} collective-permute-done((bf16[128,2048]{1,0:T(8,128)(2,1)S(1)}, bf16[128,2048]{1,0:T(8,128)(2,1)S(1)}, u32[]{:S(2)}, u32[]{:S(2)}) %collective-permute-start.17) | collective-permute-done | bytes 524320 | tf_op jit(solution)/shard_map/ppermute | solution.py:304
  157.9 3.6 %collective-permute-done.18.refs_2_ = bf16[64,2048]{1,0:T(8,128)(2,1)S(1)} collective-permute-done((bf16[64,2048]{1,0:T(8,128)(2,1)S(1)}, bf16[64,2048]{1,0:T(8,128)(2,1)S(1)}, u32[]{:S(2)}, u32[]{:S(2)}) %collective-permute-start.18) | collective-permute-done | bytes 262176 | tf_op jit(solution)/shard_map/ppermute | solution.py:304
  166.0 5.5 %collective-permute-done.19.refs_1_ = bf16[64,2048]{1,0:T(8,128)(2,1)S(1)} collective-permute-done((bf16[64,2048]{1,0:T(8,128)(2,1)S(1)}, bf16[64,2048]{1,0:T(8,128)(2,1)S(1)}, u32[]{:S(2)}, u32[]{:S(2)}) %collective-permute-start.19) | collective-permute-done | bytes 262176 | tf_op jit(solution)/shard_map/ppermute | solution.py:304
  175.4 6.4 %collective-permute-done.20.refs_1_ = bf16[128,2048]{1,0:T(8,128)(2,1)S(1)} collective-permute-done((bf16[128,2048]{1,0:T(8,128)(2,1)S(1)}, bf16[128,2048]{1,0:T(8,128)(2,1)S(1)}, u32[]{:S(2)}, u32[]{:S(2)}) %collective-permute-start.20) | collective-permute-done | bytes 524320 | tf_op jit(solution)/shard_map/ppermute | solution.py:304
  187.7 7.1 %fusion.21.refs_0_ = bf16[512,1024]{1,0:T(8,128)(2,1)S(1)} fusion(bf16[512,4096]{1,0:T(8,128)(2,1)S(1)} %shard_map.126.array_ref, bf16[4096,4008]{0,1:T(8,128)(2,1)} %param.13), kind=kOutput, calls=%fused_computation.21 | convolution fusion | flops 4295491584 | bytes 13631488 | tf_op jit(solution)/shard_map/dot_general | solution.py:369
  198.2 7.1 %fusion.24.refs_0_ = bf16[512,1024]{1,0:T(8,128)(2,1)S(1)} fusion(bf16[512,4096]{1,0:T(8,128)(2,1)S(1)} %shard_map.129.array_ref, bf16[4096,4008]{0,1:T(8,128)(2,1)} %param.13), kind=kOutput, calls=%fused_computation.22 | convolution fusion | flops 4295491584 | bytes 13631488 | tf_op jit(solution)/shard_map/dot_general | solution.py:369
  213.5 7.1 %fusion.27.refs_0_ = bf16[512,1024]{1,0:T(8,128)(2,1)S(1)} fusion(bf16[512,4096]{1,0:T(8,128)(2,1)S(1)} %shard_map.133.array_ref, bf16[4096,4008]{0,1:T(8,128)(2,1)} %param.13), kind=kOutput, calls=%fused_computation.23 | convolution fusion | flops 4295491584 | bytes 13631488 | tf_op jit(solution)/shard_map/dot_general | solution.py:369
  223.6 7.2 %fusion.18.refs_0_ = bf16[512,936]{1,0:T(8,128)(2,1)S(1)} fusion(bf16[512,4096]{1,0:T(8,128)(2,1)S(1)} %shard_map.136, bf16[4096,4008]{0,1:T(8,128)(2,1)} %param.13), kind=kOutput, calls=%fused_computation.20 | convolution fusion | flops 3926347776 | bytes 12820480 | tf_op jit(solution)/shard_map/dot_general | solution.py:369
  238.5 20.5 %collective-permute-done.32.refs_1_ = bf16[256,1024]{1,0:T(8,128)(2,1)S(1)} collective-permute-done((bf16[256,1024]{1,0:T(8,128)(2,1)S(1)}, bf16[256,1024]{1,0:T(8,128)(2,1)S(1)}, u32[]{:S(2)}, u32[]{:S(2)}) %collective-permute-start.32) | collective-permute-done | bytes 524320 | tf_op jit(solution)/shard_map/ppermute | solution.py:304
  263.9 6.5 %collective-permute-done.34.refs_1_ = bf16[128,1024]{1,0:T(8,128)(2,1)S(1)} collective-permute-done((bf16[128,1024]{1,0:T(8,128)(2,1)S(1)}, bf16[128,1024]{1,0:T(8,128)(2,1)S(1)}, u32[]{:S(2)}, u32[]{:S(2)}) %collective-permute-start.34) | collective-permute-done | bytes 262176 | tf_op jit(solution)/shard_map/ppermute | solution.py:304
  280.3 8.8 %all_gather.3 = f32[8,4,8,128]{3,2,1,0:T(8,128)S(1)} all-gather(f32[1,4,8,128]{3,2,1,0:T(8,128)S(1)} %bitcast.51), channel_id=1, replica_groups=mesh['dm'=4,'hv'=8] {'hv'}, dimensions={0}, use_global_device_ids=true | all-gather | bytes 147456 | tf_op jit(solution)/shard_map/all_gather | solution.py:397
  (165 shorter events, 104.6 us)
Async XLA Ops:
  2.3 16.3 %collective-permute-start.2 = (bf16[64,4096]{1,0:T(8,128)(2,1)S(1)}, bf16[64,4096]{1,0:T(8,128)(2,1)S(1)}, u32[]{:S(2)}, u32[]{:S(2)}) collective-permute-start(bf16[64,4096]{1,0:T(8,128)(2,1)S(1)} %broadcast_select_fusion.refs_0_), channel_id=1, source_target_pairs={{0,2},{1,3},{2,0},{3,1},{4,6},{5,7},{6,4},{7,5},{8,10},{9,11},{10,... | collective-permute-start | bytes 1572872 | tf_op jit(solution)/shard_map/ppermute | solution.py:304
  4.8 14.0 %collective-permute-start.3 = (bf16[64,4096]{1,0:T(8,128)(2,1)S(1)}, bf16[64,4096]{1,0:T(8,128)(2,1)S(1)}, u32[]{:S(2)}, u32[]{:S(2)}) collective-permute-start(bf16[64,4096]{1,0:T(8,128)(2,1)S(1)} %broadcast_select_fusion.refs_0_), channel_id=1, source_target_pairs={{0,4},{1,5},{2,6},{3,7},{4,0},{5,1},{6,2},{7,3},{8,12},{9,13},{10,... | collective-permute-start | bytes 1572872 | tf_op jit(solution)/shard_map/ppermute | solution.py:304
  19.6 16.0 %collective-permute-start.1 = (bf16[64,3328]{1,0:T(8,128)(2,1)S(1)}, bf16[64,3328]{1,0:T(8,128)(2,1)S(1)}, u32[]{:S(2)}, u32[]{:S(2)}) collective-permute-start(bf16[64,3328]{1,0:T(8,128)(2,1)S(1)} %shard_map.96.refs_2_), channel_id=1, source_target_pairs={{0,8},{1,17},{2,10},{3,19},{4,12},{5,21},{6,14},{7,23},{8,0},{9,25... | collective-permute-start | bytes 1277960 | tf_op jit(solution)/shard_map/ppermute | solution.py:304
  21.2 15.0 %collective-permute-start.6 = (bf16[64,4096]{1,0:T(8,128)(2,1)S(1)}, bf16[64,4096]{1,0:T(8,128)(2,1)S(1)}, u32[]{:S(2)}, u32[]{:S(2)}) collective-permute-start(bf16[64,4096]{1,0:T(8,128)(2,1)S(1)} %get-tuple-element.29), channel_id=1, source_target_pairs={{0,4},{1,3},{2,6},{3,1},{4,0},{5,7},{6,2},{7,5},{8,12},{9,11},{10,... | collective-permute-start | bytes 1572872 | tf_op jit(solution)/shard_map/ppermute | solution.py:304
  36.9 15.0 %collective-permute-start.5 = (bf16[64,3328]{1,0:T(8,128)(2,1)S(1)}, bf16[64,3328]{1,0:T(8,128)(2,1)S(1)}, u32[]{:S(2)}, u32[]{:S(2)}) collective-permute-start(bf16[64,3328]{1,0:T(8,128)(2,1)S(1)} %shard_map.100.refs_1_.refs_0_), channel_id=1, source_target_pairs={{0,16},{1,9},{2,18},{3,11},{4,20},{5,13},{6,22},{7,15},{8,24},{9,1... | collective-permute-start | bytes 1277960 | tf_op jit(solution)/shard_map/ppermute | solution.py:304
  39.5 38.0 %collective-permute-start.9 = (bf16[128,3328]{1,0:T(8,128)(2,1)S(1)}, bf16[128,3328]{1,0:T(8,128)(2,1)S(1)}, u32[]{:S(2)}, u32[]{:S(2)}) collective-permute-start(bf16[128,3328]{1,0:T(8,128)(2,1)S(1)} %shard_map.99.refs_3_), channel_id=1, source_target_pairs={{0,16},{1,9},{2,18},{3,11},{4,20},{5,13},{6,22},{7,15},{8,24},{9,1... | collective-permute-start | bytes 2555912 | tf_op jit(solution)/shard_map/ppermute | solution.py:304
  50.4 35.3 %collective-permute-start.11 = (bf16[64,3328]{1,0:T(8,128)(2,1)S(1)}, bf16[64,3328]{1,0:T(8,128)(2,1)S(1)}, u32[]{:S(2)}, u32[]{:S(2)}) collective-permute-start(bf16[64,3328]{1,0:T(8,128)(2,1)S(1)} %shard_map.103.refs_2_), channel_id=1, source_target_pairs={{0,8},{1,17},{2,10},{3,19},{4,12},{5,21},{6,14},{7,23},{8,0},{9,25... | collective-permute-start | bytes 1277960 | tf_op jit(solution)/shard_map/ppermute | solution.py:304
  78.3 20.3 %collective-permute-start.10 = (bf16[64,3328]{1,0:T(8,128)(2,1)S(1)}, bf16[64,3328]{1,0:T(8,128)(2,1)S(1)}, u32[]{:S(2)}, u32[]{:S(2)}) collective-permute-start(bf16[64,3328]{1,0:T(8,128)(2,1)S(1)} %get-tuple-element.31), channel_id=1, source_target_pairs={{0,8},{1,17},{2,10},{3,19},{4,12},{5,21},{6,14},{7,23},{8,0},{9,25... | collective-permute-start | bytes 1277960 | tf_op jit(solution)/shard_map/ppermute | solution.py:304
  86.4 19.9 %collective-permute-start.13 = (bf16[64,3328]{1,0:T(8,128)(2,1)S(1)}, bf16[64,3328]{1,0:T(8,128)(2,1)S(1)}, u32[]{:S(2)}, u32[]{:S(2)}) collective-permute-start(bf16[64,3328]{1,0:T(8,128)(2,1)S(1)} %shard_map.106.refs_2_.refs_0_), channel_id=1, source_target_pairs={{0,16},{1,9},{2,18},{3,11},{4,20},{5,13},{6,22},{7,15},{8,24},{9,1... | collective-permute-start | bytes 1277960 | tf_op jit(solution)/shard_map/ppermute | solution.py:304
  89.9 12.1 %collective-permute-start.8 = (bf16[64,1664]{1,0:T(8,128)(2,1)S(1)}, bf16[64,1664]{1,0:T(8,128)(2,1)S(1)}, u32[]{:S(2)}, u32[]{:S(2)}) collective-permute-start(bf16[64,1664]{1,0:T(8,128)(2,1)S(1)} %shard_map.104.refs_3_.refs_0_), channel_id=1, source_target_pairs={{0,8},{1,17},{2,10},{3,19},{4,12},{5,21},{6,14},{7,23},{8,0},{9,25... | collective-permute-start | bytes 638984 | tf_op jit(solution)/shard_map/ppermute | solution.py:304
  109.1 15.6 %collective-permute-start.14 = (bf16[128,1664]{1,0:T(8,128)(2,1)S(1)}, bf16[128,1664]{1,0:T(8,128)(2,1)S(1)}, u32[]{:S(2)}, u32[]{:S(2)}) collective-permute-start(bf16[128,1664]{1,0:T(8,128)(2,1)S(1)} %shard_map.110.refs_1_), channel_id=1, source_target_pairs={{0,16},{1,9},{2,18},{3,11},{4,20},{5,13},{6,22},{7,15},{8,24},{9,1... | collective-permute-start | bytes 1277960 | tf_op jit(solution)/shard_map/ppermute | solution.py:304
  109.7 10.1 %collective-permute-start.15 = (bf16[64,1664]{1,0:T(8,128)(2,1)S(1)}, bf16[64,1664]{1,0:T(8,128)(2,1)S(1)}, u32[]{:S(2)}, u32[]{:S(2)}) collective-permute-start(bf16[64,1664]{1,0:T(8,128)(2,1)S(1)} %shard_map.109.refs_2_.refs_3_), channel_id=1, source_target_pairs={{0,8},{1,17},{2,10},{3,19},{4,12},{5,21},{6,14},{7,23},{8,0},{9,25... | collective-permute-start | bytes 638984 | tf_op jit(solution)/shard_map/ppermute | solution.py:304
  139.0 15.4 %collective-permute-start.17 = (bf16[128,2048]{1,0:T(8,128)(2,1)S(1)}, bf16[128,2048]{1,0:T(8,128)(2,1)S(1)}, u32[]{:S(2)}, u32[]{:S(2)}) collective-permute-start(bf16[128,2048]{1,0:T(8,128)(2,1)S(1)} %get-tuple-element.33), channel_id=1, source_target_pairs={{0,2},{1,5},{2,0},{3,7},{4,6},{5,1},{6,4},{7,3},{8,10},{9,13},{10,... | collective-permute-start | bytes 1572872 | tf_op jit(solution)/shard_map/ppermute | solution.py:304
  146.6 9.8 %collective-permute-start.23 = (bf16[64,2048]{1,0:T(8,128)(2,1)S(1)}, bf16[64,2048]{1,0:T(8,128)(2,1)S(1)}, u32[]{:S(2)}, u32[]{:S(2)}) collective-permute-start(bf16[64,2048]{1,0:T(8,128)(2,1)S(1)} %get-tuple-element.40), channel_id=1, source_target_pairs={{0,4},{1,3},{2,6},{3,1},{4,0},{5,7},{6,2},{7,5},{8,12},{9,11},{10,... | collective-permute-start | bytes 786440 | tf_op jit(solution)/shard_map/ppermute | solution.py:304
  187.6 9.8 %collective-permute-start.28 = (f32[256,128]{1,0:T(8,128)S(1)}, f32[256,128]{1,0:T(8,128)S(1)}, u32[]{:S(2)}, u32[]{:S(2)}) collective-permute-start(f32[256,128]{1,0:T(8,128)S(1)} %shard_map.125.after_ref), channel_id=1, source_target_pairs={{0,8},{1,17},{2,10},{3,19},{4,12},{5,21},{6,14},{7,23},{8,0},{9,25... | collective-permute-start | bytes 393224 | tf_op jit(solution)/shard_map/ppermute | solution.py:304
  195.4 17.4 %collective-permute-start.29 = (bf16[256,1024]{1,0:T(8,128)(2,1)S(1)}, bf16[256,1024]{1,0:T(8,128)(2,1)S(1)}, u32[]{:S(2)}, u32[]{:S(2)}) collective-permute-start(bf16[256,1024]{1,0:T(8,128)(2,1)S(1)} %shard_map.127.refs_2_), channel_id=1, source_target_pairs={{0,8},{1,17},{2,10},{3,19},{4,12},{5,21},{6,14},{7,23},{8,0},{9,25... | collective-permute-start | bytes 1572872 | tf_op jit(solution)/shard_map/ppermute | solution.py:304
  198.0 13.1 %collective-permute-start.30 = (f32[128,128]{1,0:T(8,128)S(1)}, f32[128,128]{1,0:T(8,128)S(1)}, u32[]{:S(2)}, u32[]{:S(2)}) collective-permute-start(f32[128,128]{1,0:T(8,128)S(1)} %get-tuple-element.45), channel_id=1, source_target_pairs={{0,16},{1,9},{2,18},{3,11},{4,20},{5,13},{6,22},{7,15},{8,24},{9,1... | collective-permute-start | bytes 196616 | tf_op jit(solution)/shard_map/ppermute | solution.py:304
  205.8 17.0 %collective-permute-start.31 = (bf16[256,1024]{1,0:T(8,128)(2,1)S(1)}, bf16[256,1024]{1,0:T(8,128)(2,1)S(1)}, u32[]{:S(2)}, u32[]{:S(2)}) collective-permute-start(bf16[256,1024]{1,0:T(8,128)(2,1)S(1)} %shard_map.130.refs_2_), channel_id=1, source_target_pairs={{0,8},{1,17},{2,10},{3,19},{4,12},{5,21},{6,14},{7,23},{8,0},{9,25... | collective-permute-start | bytes 1572872 | tf_op jit(solution)/shard_map/ppermute | solution.py:304
  221.2 15.0 %collective-permute-start.33 = (bf16[256,1024]{1,0:T(8,128)(2,1)S(1)}, bf16[256,1024]{1,0:T(8,128)(2,1)S(1)}, u32[]{:S(2)}, u32[]{:S(2)}) collective-permute-start(bf16[256,1024]{1,0:T(8,128)(2,1)S(1)} %shard_map.134.refs_2_), channel_id=1, source_target_pairs={{0,8},{1,17},{2,10},{3,19},{4,12},{5,21},{6,14},{7,23},{8,0},{9,25... | collective-permute-start | bytes 1572872 | tf_op jit(solution)/shard_map/ppermute | solution.py:304
  231.4 27.6 %collective-permute-start.32 = (bf16[256,1024]{1,0:T(8,128)(2,1)S(1)}, bf16[256,1024]{1,0:T(8,128)(2,1)S(1)}, u32[]{:S(2)}, u32[]{:S(2)}) collective-permute-start(bf16[256,1024]{1,0:T(8,128)(2,1)S(1)} %shard_map.137.refs_2_), channel_id=1, source_target_pairs={{0,8},{1,17},{2,10},{3,19},{4,12},{5,21},{6,14},{7,23},{8,0},{9,25... | collective-permute-start | bytes 1572872 | tf_op jit(solution)/shard_map/ppermute | solution.py:304
  233.3 26.9 %collective-permute-start.35 = (bf16[128,1024]{1,0:T(8,128)(2,1)S(1)}, bf16[128,1024]{1,0:T(8,128)(2,1)S(1)}, u32[]{:S(2)}, u32[]{:S(2)}) collective-permute-start(bf16[128,1024]{1,0:T(8,128)(2,1)S(1)} %get-tuple-element.51), channel_id=1, source_target_pairs={{0,16},{1,9},{2,18},{3,11},{4,20},{5,13},{6,22},{7,15},{8,24},{9,1... | collective-permute-start | bytes 786440 | tf_op jit(solution)/shard_map/ppermute | solution.py:304
  234.2 25.9 %collective-permute-start.36 = (bf16[128,1024]{1,0:T(8,128)(2,1)S(1)}, bf16[128,1024]{1,0:T(8,128)(2,1)S(1)}, u32[]{:S(2)}, u32[]{:S(2)}) collective-permute-start(bf16[128,1024]{1,0:T(8,128)(2,1)S(1)} %get-tuple-element.52), channel_id=1, source_target_pairs={{0,16},{1,9},{2,18},{3,11},{4,20},{5,13},{6,22},{7,15},{8,24},{9,1... | collective-permute-start | bytes 786440 | tf_op jit(solution)/shard_map/ppermute | solution.py:304
  236.9 25.5 %collective-permute-start.37 = (bf16[128,1024]{1,0:T(8,128)(2,1)S(1)}, bf16[128,1024]{1,0:T(8,128)(2,1)S(1)}, u32[]{:S(2)}, u32[]{:S(2)}) collective-permute-start(bf16[128,1024]{1,0:T(8,128)(2,1)S(1)} %get-tuple-element.53), channel_id=1, source_target_pairs={{0,16},{1,9},{2,18},{3,11},{4,20},{5,13},{6,22},{7,15},{8,24},{9,1... | collective-permute-start | bytes 786440 | tf_op jit(solution)/shard_map/ppermute | solution.py:304
  259.7 10.7 %collective-permute-start.34 = (bf16[128,1024]{1,0:T(8,128)(2,1)S(1)}, bf16[128,1024]{1,0:T(8,128)(2,1)S(1)}, u32[]{:S(2)}, u32[]{:S(2)}) collective-permute-start(bf16[128,1024]{1,0:T(8,128)(2,1)S(1)} %get-tuple-element.50), channel_id=1, source_target_pairs={{0,16},{1,9},{2,18},{3,11},{4,20},{5,13},{6,22},{7,15},{8,24},{9,1... | collective-permute-start | bytes 786440 | tf_op jit(solution)/shard_map/ppermute | solution.py:304
  (30 other events, 798.5 us)
